TPU v7x, 256 devices: a whole 4x4x8 slice. The times are simulated.
256 devices in a mesh: gx: 8 (over z), gy: 4 (over x), gz: 8 (over y, core).
Axes of the slice: x: 4, y: 4, z: 8, core: 2. Of those that a mesh axis runs over, the one named last changes fastest.
Arguments:
- positions: float32 [3, 12288, 512], P(None, ('gx', 'gy', 'gz')), may hold values from -1 to 1
- spacing: float32 [12288, 8], P(('gx', 'gy', 'gz')), may hold values from 0.0005 to 0.02
- crossings: int32 [12288, 8], P(('gx', 'gy', 'gz')), may hold values from 0 to 255, all different within a row; in each aligned block of 48 rows (0 to 47, 48 to 95, ...) at most 3 rows name the same one
- target: float32 [3, 12288], P(None, ('gx', 'gy', 'gz')), may hold values from 0 to 1
- first_weight: bfloat16 [256, 256, 60], P(('gx', 'gy', 'gz')), may hold values from -0.75 to 0.75
- head_weight: bfloat16 [256, 4, 256], P(('gx', 'gy', 'gz')), may hold values from -0.375 to 0.375
Outputs:
- rendered: float32 [3, 12288], P(None, ('gx', 'gy', 'gz'))
- first_update: float32 [256, 256, 60], P(('gx', 'gy', 'gz'))
- head_update: float32 [256, 4, 256], P(('gx', 'gy', 'gz'))
Inputs may be any that keep to these rules, and one draw needn't show every extreme that they name: `crossings`: each ray crosses 8 different bricks, in no spatial pattern over the devices. Among the rays of one device no brick is crossed more than 3 times, a bound that some block reaches.
All inputs are finite; a program needn't handle non-finite values.
Results may differ from a plain program's by a relative error of at most 0.0029.
Values sent between devices are 32-bit elements; how exact they have to be, the bound alone decides.
No kernel may reach another device: no remote copies, remote signals or barrier semaphores. Data moves between devices by JAX's collectives and lax.ppermute only.
A program may use at most 64 MiB of HBM per device.

v0:
```python
import math

import jax
import jax.numpy as jnp
from jax import lax
from jax.sharding import PartitionSpec as P

FREQS = 10
SAMPLES = 64
SEGS = 8


PI_VALUE = 3.141592653589793
NORM_EPS = 1e-06
BLOCK_LIMIT = 2048


def encode(points):
    scales = 2.0 ** jnp.arange(FREQS, dtype=jnp.float32) * PI_VALUE
    angles = scales[:, None, None] * points[None]
    wave_table = jnp.stack([jnp.sin(angles), jnp.cos(angles)], axis=1)
    return wave_table.reshape(6 * FREQS, points.shape[1]).astype(jnp.bfloat16)


def network(first_local, head_local, points):
    encoded = encode(points)
    before = jnp.dot(first_local, encoded, preferred_element_type=jnp.float32)
    hidden = jax.nn.silu(before).astype(jnp.bfloat16)
    output = jnp.dot(head_local, hidden, preferred_element_type=jnp.float32)
    return (encoded, before, hidden, output)


def activate(output):
    return (jax.nn.softplus(output[0]), jax.nn.sigmoid(output[1:]))


def segment_forward(density, colour, step_len):
    optical = density * step_len[:, None]
    inclusive = jnp.cumsum(optical, axis=1)
    leaving = jnp.exp(-inclusive)
    weight = jnp.exp(optical - inclusive) - leaving
    seg_colour = jnp.sum(weight[None] * colour, axis=2)
    return (seg_colour, leaving[:, -1], weight, leaving)


def segment_backward(colour, weight, leaving, step_len, grad_colour, grad_trans):
    shading = jnp.sum(colour * grad_colour[:, :, None], axis=0)
    weighted = weight * shading
    after = jnp.sum(weighted, axis=1, keepdims=True) - jnp.cumsum(weighted, axis=1)
    grad_depth = shading * leaving - after - (grad_trans * leaving[:, -1])[:, None]
    grad_density = grad_depth * step_len[:, None]
    grad_sample = weight[None] * grad_colour[:, :, None]
    return (grad_density, grad_sample)


def ray_level(seg_colour, seg_trans, target):
    seg_total = seg_trans.shape[1]
    through = jnp.cumprod(seg_trans, axis=1)
    prefix = jnp.concatenate([jnp.ones_like(seg_trans[:, :1]), through[:, :-1]], axis=1)
    rendered = jnp.sum(prefix[None] * seg_colour, axis=2)
    residual = rendered - target
    grad_colour = prefix[None] * residual[:, :, None]
    behind_list = [jnp.zeros_like(rendered)]
    for offset in range(seg_total - 1, 0, -1):
        behind_list.append(seg_colour[:, :, offset] + seg_trans[:, offset][None] * behind_list[-1])
    behind = jnp.stack(behind_list[::-1], axis=2)
    grad_trans = prefix * jnp.sum(behind * residual[:, :, None], axis=0)
    return (rendered, grad_colour, grad_trans)


def output_grad(output, grad_density, grad_sample):
    colour = jax.nn.sigmoid(output[1:])
    first_row = grad_density * jax.nn.sigmoid(output[0])
    others = grad_sample * colour * (1.0 - colour)
    return jnp.concatenate([first_row[None], others], axis=0).astype(jnp.bfloat16)


def network_grad(head_local, encoded, before, hidden, upstream):
    grad_head = lax.dot_general(
        upstream, hidden, (((1,), (1,)), ((), ())), preferred_element_type=jnp.float32
    )
    grad_hidden = lax.dot_general(
        head_local, upstream, (((0,), (0,)), ((), ())), preferred_element_type=jnp.float32
    )
    logistic = jax.nn.sigmoid(before)
    grad_before = (grad_hidden * logistic * (1.0 + before * (1.0 - logistic))).astype(jnp.bfloat16)
    grad_first = lax.dot_general(
        grad_before, encoded, (((1,), (1,)), ((), ())), preferred_element_type=jnp.float32
    )
    return (grad_first, grad_head)


def on_device(positions, spacing, crossings, target, first_weight, head_weight):
    across = lax.axis_size(("gx", "gy"))
    along_count = lax.axis_size("gz")
    devices = across * along_count
    ray_rows = crossings.shape[0]
    entries = ray_rows * SEGS
    capacity = 2 * entries // devices
    total_slots = devices * capacity
    sample_total = total_slots * SAMPLES
    block_size = math.gcd(sample_total, BLOCK_LIMIT)
    block_count = sample_total // block_size
    block_segs = block_size // SAMPLES
    first_local = first_weight[0]
    head_local = head_weight[0]
    brick_ids = crossings.reshape(entries)
    order_rank = jnp.arange(entries, dtype=jnp.int32)
    earlier = (brick_ids[:, None] == brick_ids[None, :]) & (
        order_rank[None, :] < order_rank[:, None]
    )
    column = brick_ids * capacity + jnp.sum(earlier.astype(jnp.int32), axis=1)
    own_points = positions.reshape(3, entries, SAMPLES)
    own_steps = spacing.reshape(entries)
    send_points = jnp.zeros((3, total_slots, SAMPLES), jnp.float32).at[:, column, :].set(own_points)
    send_steps = jnp.zeros((1, total_slots), jnp.float32).at[0, column].set(own_steps)
    got_points, got_steps = (
        lax.all_to_all(
            lax.all_to_all(
                send_points.reshape(3, across, along_count, capacity * SAMPLES),
                ("gx", "gy"),
                split_axis=1,
                concat_axis=1,
                tiled=True,
            ),
            "gz",
            split_axis=2,
            concat_axis=2,
            tiled=True,
        ),
        lax.all_to_all(
            lax.all_to_all(
                send_steps.reshape(1, across, along_count, capacity),
                ("gx", "gy"),
                split_axis=1,
                concat_axis=1,
                tiled=True,
            ),
            "gz",
            split_axis=2,
            concat_axis=2,
            tiled=True,
        ),
    )
    point_blocks = got_points.reshape(3, block_count, block_size).transpose(1, 0, 2)
    step_blocks = got_steps.reshape(block_count, block_segs)

    def forward_turn(unused, inputs):
        block_points, block_steps = inputs
        encoded, before, hidden, output = network(first_local, head_local, block_points)
        density, colour = activate(output)
        result = jnp.concatenate([density[None], colour], axis=0)
        return (unused, result)

    unused, results = lax.scan(
        forward_turn, jnp.zeros((), jnp.float32), (point_blocks, step_blocks)
    )
    values = results.transpose(1, 0, 2).reshape(4, across, along_count, capacity * SAMPLES)
    returned = lax.all_to_all(
        lax.all_to_all(values, ("gx", "gy"), split_axis=1, concat_axis=1, tiled=True),
        "gz",
        split_axis=2,
        concat_axis=2,
        tiled=True,
    )
    owned = returned.reshape(4, total_slots, SAMPLES)[:, column, :]
    seg_colour, seg_trans, weight, leaving = segment_forward(owned[0], owned[1:], own_steps)
    rendered, grad_colour, grad_trans = ray_level(
        seg_colour.reshape(3, ray_rows, SEGS), seg_trans.reshape(ray_rows, SEGS), target
    )
    grad_density, grad_sample = segment_backward(
        owned[1:],
        weight,
        leaving,
        own_steps,
        grad_colour.reshape(3, entries),
        grad_trans.reshape(entries),
    )
    stacked = jnp.concatenate([grad_density[None], grad_sample], axis=0)
    send_grads = jnp.zeros((4, total_slots, SAMPLES), jnp.float32).at[:, column, :].set(stacked)
    got_grads = lax.all_to_all(
        lax.all_to_all(
            send_grads.reshape(4, across, along_count, capacity * SAMPLES),
            ("gx", "gy"),
            split_axis=1,
            concat_axis=1,
            tiled=True,
        ),
        "gz",
        split_axis=2,
        concat_axis=2,
        tiled=True,
    )
    grad_blocks = got_grads.reshape(4, block_count, block_size).transpose(1, 0, 2)

    def backward_turn(totals, inputs):
        block_points, block_steps, block_upstream = inputs
        encoded, before, hidden, output = network(first_local, head_local, block_points)
        grad_density = block_upstream[0]
        grad_sample = block_upstream[1:]
        upstream = output_grad(output, grad_density, grad_sample)
        grad_first, grad_head = network_grad(head_local, encoded, before, hidden, upstream)
        return ((totals[0] + grad_first, totals[1] + grad_head), None)

    start_totals = (
        jnp.zeros(first_local.shape, jnp.float32),
        jnp.zeros(head_local.shape, jnp.float32),
    )
    totals, unused_out = lax.scan(
        backward_turn, start_totals, (point_blocks, step_blocks, grad_blocks)
    )
    grad_first, grad_head = totals
    square_sum = jnp.sum(grad_first * grad_first) + jnp.sum(grad_head * grad_head)
    overall = lax.psum(square_sum, ("gx", "gy", "gz"))
    count_all = devices * (grad_first.size + grad_head.size)
    scale = lax.rsqrt(overall / count_all + NORM_EPS)
    return (rendered, (grad_first * scale)[None], (grad_head * scale)[None])


def solution(mesh):
    in_specs = (
        P(None, ("gx", "gy", "gz"), None),
        P(("gx", "gy", "gz"), None),
        P(("gx", "gy", "gz"), None),
        P(None, ("gx", "gy", "gz")),
        P(("gx", "gy", "gz"), None, None),
        P(("gx", "gy", "gz"), None, None),
    )
    out_specs = (
        P(None, ("gx", "gy", "gz")),
        P(("gx", "gy", "gz"), None, None),
        P(("gx", "gy", "gz"), None, None),
    )
    return jax.shard_map(
        on_device, mesh=mesh, in_specs=in_specs, out_specs=out_specs, check_vma=False
    )
```

profile of v0, /device:TPU:1, one launch (start us, length us, event | category | flops | bytes accessed | tf_op | source)
XLA Modules:
  0.0 600.6 jit_solution(16509531999014523574)
XLA Ops:
  4.3 11.8 %scatter_fusion = f32[3,768,64]{2,0,1:T(4,128)S(1)} fusion(f32[3,768,64]{2,0,1:T(4,128)S(1)} %broadcast_in_dim.24, s32[384]{0:T(512)S(1)} %fusion.38, f32[384,3,64]{2,1,0:T(4,128)S(1)} %copy.150), kind=kCustom, calls=%fused_computation.1 | custom fusion | bytes 886272 | tf_op jit(solution)/shard_map/scatter | solution.py:115
  16.8 32.7 %all_to_all.30 = f32[3,32,8,192]{3,2,0,1:T(8,128)S(1)} all-to-all(f32[3,32,8,192]{3,2,0,1:T(8,128)S(1)} %copy.152), channel_id=1, replica_groups=mesh['gx'=8,'gy'=4,'gz'=8] {'gx','gy'}, dimensions={1} | all-to-all | bytes 1179648 | tf_op jit(solution)/shard_map/all_to_all | solution.py:119
  50.7 7.3 %all-to-all-start.1 = ((f32[3,32,8,192]{3,1,0,2:T(8,128)}), f32[3,32,8,192]{3,1,0,2:T(8,128)S(1)}, u32[]{:S(2)}, u32[]{:S(2)}) async-start(f32[3,32,8,192]{3,1,0,2:T(8,128)} %copy.153), calls=%async_computation.1 | async-start | bytes 1572864 | tf_op jit(solution)/shard_map/all_to_all | solution.py:118
  58.1 12.2 %all-to-all-done.1 = f32[3,32,8,192]{3,1,0,2:T(8,128)S(1)} async-done(((f32[3,32,8,192]{3,1,0,2:T(8,128)}), f32[3,32,8,192]{3,1,0,2:T(8,128)S(1)}, u32[]{:S(2)}, u32[]{:S(2)}) %all-to-all-start.1) | async-done | bytes 589856 | tf_op jit(solution)/shard_map/all_to_all | solution.py:118
  71.6 95.6 %while.23 = (s32[]{:T(128)}, f32[24,4,2048]{2,1,0:T(4,128)S(1)}, f32[24,3,2048]{2,1,0:T(4,128)S(1)}, bf16[256,60]{1,0:T(8,128)(2,1)S(1)}, bf16[4,256]{1,0:T(4,128)(2,1)S(1)}, /*index=5*/s32[]{:T(128)}) while((s32[]{:T(128)}, f32[24,4,2048]{2,1,0:T(4,128)S(1)}, f32[24,3,2048]{2,1,0:T(4,128)S(1)}, bf16[256,60]{1,0:T(8,128)(2,1)S(1)}, ...), condition=%wide.region_3.4_spmd, body=%wide.region_2.3_spmd.sunk | while | flops 70076424 | bytes 1753245 | solution.py:155
  169.4 30.6 %all_to_all.31 = f32[4,32,8,192]{3,2,0,1:T(8,128)S(1)} all-to-all(f32[4,32,8,192]{3,2,0,1:T(8,128)S(1)} %copy.158), channel_id=1, replica_groups=mesh['gx'=8,'gy'=4,'gz'=8] {'gx','gy'}, dimensions={1} | all-to-all | bytes 1572864 | tf_op jit(solution)/shard_map/all_to_all | solution.py:160
  201.6 6.4 %all-to-all-start.3 = ((f32[4,32,8,192]{3,1,0,2:T(8,128)}), f32[4,32,8,192]{3,1,0,2:T(8,128)S(1)}, u32[]{:S(2)}, u32[]{:S(2)}) async-start(f32[4,32,8,192]{3,1,0,2:T(8,128)} %copy.159), calls=%async_computation.3 | async-start | bytes 2097152 | tf_op jit(solution)/shard_map/all_to_all | solution.py:159
  208.3 14.9 %all-to-all-done.3 = f32[4,32,8,192]{3,1,0,2:T(8,128)S(1)} async-done(((f32[4,32,8,192]{3,1,0,2:T(8,128)}), f32[4,32,8,192]{3,1,0,2:T(8,128)S(1)}, u32[]{:S(2)}, u32[]{:S(2)}) %all-to-all-start.3) | async-done | bytes 786464 | tf_op jit(solution)/shard_map/all_to_all | solution.py:159
  231.0 11.8 %scatter_fusion.1 = f32[4,768,64]{2,0,1:T(4,128)S(1)} fusion(f32[4,768,64]{2,0,1:T(4,128)S(1)} %broadcast_in_dim.27, s32[384]{0:T(512)S(1)} %fusion.38, f32[384,4,64]{2,1,0:T(4,128)S(1)} %copy.176), kind=kCustom, calls=%fused_computation.2 | custom fusion | bytes 1181184 | tf_op jit(solution)/shard_map/scatter | solution.py:180
  243.7 31.1 %all_to_all.32 = f32[4,32,8,192]{3,2,0,1:T(8,128)S(1)} all-to-all(f32[4,32,8,192]{3,2,0,1:T(8,128)S(1)} %copy.178), channel_id=1, replica_groups=mesh['gx'=8,'gy'=4,'gz'=8] {'gx','gy'}, dimensions={1} | all-to-all | bytes 1572864 | tf_op jit(solution)/shard_map/all_to_all | solution.py:182
  276.5 6.4 %all-to-all-start.5 = ((f32[4,32,8,192]{3,1,0,2:T(8,128)}), f32[4,32,8,192]{3,1,0,2:T(8,128)S(1)}, u32[]{:S(2)}, u32[]{:S(2)}) async-start(f32[4,32,8,192]{3,1,0,2:T(8,128)} %copy.179), calls=%async_computation.5 | async-start | bytes 2097152 | tf_op jit(solution)/shard_map/all_to_all | solution.py:181
  282.9 15.1 %all-to-all-done.5 = f32[4,32,8,192]{3,1,0,2:T(8,128)S(1)} async-done(((f32[4,32,8,192]{3,1,0,2:T(8,128)}), f32[4,32,8,192]{3,1,0,2:T(8,128)S(1)}, u32[]{:S(2)}, u32[]{:S(2)}) %all-to-all-start.5) | async-done | bytes 786464 | tf_op jit(solution)/shard_map/all_to_all | solution.py:181
  299.2 222.5 %while.24 = (s32[]{:T(128)}, f32[256,60]{0,1:T(8,128)S(1)}, f32[4,256]{1,0:T(4,128)S(1)}, f32[24,4,2048]{2,0,1:T(8,128)S(1)}, f32[24,3,2048]{2,1,0:T(4,128)}, /*...) while((s32[]{:T(128)}, f32[256,60]{0,1:T(8,128)S(1)}, ...), condition=%wide.region_14.15_spmd.clone, body=%wide.region_13.14_spmd.clone.sunk | while | flops 146210832 | bytes 9496796 | solution.py:209
  305.8 2.7 fusion.83
  324.3 2.7 fusion.83
  333.6 2.7 fusion.83
  342.9 2.7 fusion.83
  352.1 2.7 fusion.83
  361.4 2.7 fusion.83
  370.7 2.7 fusion.83
  379.9 2.7 fusion.83
  389.2 2.7 fusion.83
  398.5 2.7 fusion.83
  407.8 2.7 fusion.83
  417.0 2.7 fusion.83
  426.3 2.7 fusion.83
  435.6 2.7 fusion.83
  444.8 2.7 fusion.83
  454.1 2.7 fusion.83
  463.4 2.7 fusion.83
  472.7 2.7 fusion.83
  524.3 74.3 %psum.7 = f32[]{:T(128)} all-reduce(f32[]{:T(128)S(6)} %add.128), channel_id=1, replica_groups=mesh['gx'=8,'gy'=4,'gz'=8] {'gx','gy','gz'}, use_global_device_ids=true, to_apply=%region_17.18 | all-reduce | flops 1 | bytes 8 | tf_op jit(solution)/shard_map/psum | solution.py:214
  (585 shorter events, 290.3 us)
Async XLA Ops:
  16.8 41.2 %copy-start.2 = (bf16[1,256,60]{1,2,0:T(8,128)(2,1)S(1)}, bf16[1,256,60]{1,2,0:T(8,128)(2,1)}, u32[]{:S(2)}) copy-start(bf16[1,256,60]{1,2,0:T(8,128)(2,1)} %param.14) | copy-start | bytes 92164
  50.7 19.6 %all-to-all-start.1 = ((f32[3,32,8,192]{3,1,0,2:T(8,128)}), f32[3,32,8,192]{3,1,0,2:T(8,128)S(1)}, u32[]{:S(2)}, u32[]{:S(2)}) async-start(f32[3,32,8,192]{3,1,0,2:T(8,128)} %copy.153), calls=%async_computation.1 | async-start | bytes 1572864 | tf_op jit(solution)/shard_map/all_to_all | solution.py:118
  58.1 13.5 %copy-start.1 = (bf16[1,4,256]{2,1,0:T(4,128)(2,1)S(1)}, bf16[1,4,256]{2,1,0:T(4,128)(2,1)}, u32[]{:S(2)}) copy-start(bf16[1,4,256]{2,1,0:T(4,128)(2,1)} %param.15) | copy-start | bytes 6148
  167.2 0.9 copy-start
  200.0 8.1 %copy-start.4 = (f32[48,8]{0,1:T(8,128)S(1)}, f32[48,8]{0,1:T(8,128)}, u32[]{:S(2)}) copy-start(f32[48,8]{0,1:T(8,128)} %param.11) | copy-start | bytes 4612
  201.6 21.6 %all-to-all-start.3 = ((f32[4,32,8,192]{3,1,0,2:T(8,128)}), f32[4,32,8,192]{3,1,0,2:T(8,128)S(1)}, u32[]{:S(2)}, u32[]{:S(2)}) async-start(f32[4,32,8,192]{3,1,0,2:T(8,128)} %copy.159), calls=%async_computation.3 | async-start | bytes 2097152 | tf_op jit(solution)/shard_map/all_to_all | solution.py:159
  227.2 1.8 copy-start.5
  228.4 2.1 copy-start.3
  276.5 21.6 %all-to-all-start.5 = ((f32[4,32,8,192]{3,1,0,2:T(8,128)}), f32[4,32,8,192]{3,1,0,2:T(8,128)S(1)}, u32[]{:S(2)}, u32[]{:S(2)}) async-start(f32[4,32,8,192]{3,1,0,2:T(8,128)} %copy.179), calls=%async_computation.5 | async-start | bytes 2097152 | tf_op jit(solution)/shard_map/all_to_all | solution.py:181
where the time goes:
time: 604 us; the launch traced here: 601 us
  blocking collectives  169 us (28%)
  matrix products  150 us (25%)
  other arithmetic  139 us (23%)
  local copies, waits for them, and re-layouts  74 us (12%)
  waiting for transfers between devices  42.2 us (7%)
  starting transfers between devices  20.2 us (3%)
    another operation x96, other arithmetic  122 us
    psum x1, blocking collectives, on_device(): overall = lax.psum(square_sum, ('gx', 'gy', 'gz'))  74.3 us
    dot_general x24, matrix products, network_grad(): lax.dot_general(grad_before, encoded, (((1,), (1,)), ((), ())), preferred...  65.6 us
    dot_general x24, matrix products, network(): before = jnp.dot(first_local, encoded, preferred_element_type=jnp.float32)  48.8 us
    all_to_all x1, blocking collectives, on_device(): lax.all_to_all(send_points.reshape(3, across, along_count, capacity * SAM...  32.7 us
    all_to_all x1, blocking collectives, on_device(): lax.all_to_all(send_grads.reshape(4, across, along_count, capacity * SAMP...  31.1 us
    all_to_all x1, blocking collectives, on_device(): lax.all_to_all(values, ('gx', 'gy'), split_axis=1, concat_axis=1, tiled=T...  30.6 us
    dot_general x48, matrix products, network(): output = jnp.dot(head_local, hidden, preferred_element_type=jnp.float32)  29.3 us
  transfers between devices with their start and end apart: 3, of which 3 were waited for; matrix products, arithmetic and copies ran while one was open for 0% of the time, Pallas kernels for 0%

commit v1 on v0

v1 whole, which is shorter than its diff:
```python
import jax
import jax.numpy as jnp
from jax import lax
from jax.experimental import pallas as pl
from jax.experimental.pallas import tpu as pltpu
from jax.sharding import PartitionSpec as P

FREQS = 10
SAMPLES = 64
SEGS = 8
CAP = 3
NORM_EPS = 1e-06

RAYS = 48
GROUP = 8
PEERS = 32
SLOTS = GROUP * CAP
PAIRS = SLOTS // 2
ROWS = PEERS // 2
TILE = PEERS * SAMPLES
ENTRIES = RAYS * SEGS
STEP_ROW = 3 * PAIRS
WIRE = 40
HIDDEN = 256
FORWARD_CHUNK = 1024
BACKWARD_CHUNK = 256
VMEM = 56 * 1024 * 1024
ALL = ("gx", "gy", "gz")
PEER_AXES = ("gx", "gy")

SIN_TERMS = (
    6.283185160116253,
    -41.34165503574907,
    81.60100428250003,
    -76.54978619700827,
    39.536730859838705,
)

f32 = jnp.float32
bf16 = jnp.bfloat16


def iota(shape, dim):
    return lax.broadcasted_iota(jnp.int32, shape, dim)


def exact_dot(a, b):
    return jnp.dot(a, b, preferred_element_type=f32, precision=lax.Precision.HIGHEST)


def nt_dot(a, b, precision=None):
    return lax.dot_general(
        a, b, (((1,), (1,)), ((), ())), preferred_element_type=f32, precision=precision
    )


def matrix_cost(tile_passes):
    return pl.CostEstimate(
        flops=tile_passes * 2 * HIDDEN * HIDDEN * TILE, bytes_accessed=4 << 20, transcendentals=0
    )


def split3(x):
    high = x.astype(bf16)
    rest = x - high.astype(f32)
    mid = rest.astype(bf16)
    return high, mid, (rest - mid.astype(f32)).astype(bf16)


def pick(one_hot, x):
    high, mid, low = split3(x)
    total = jnp.dot(one_hot, low, preferred_element_type=f32)
    total += jnp.dot(one_hot, mid, preferred_element_type=f32)
    return total + jnp.dot(one_hot, high, preferred_element_type=f32)


def column_of(rows_ref):
    rows = rows_ref[...].astype(f32)
    padded = jnp.concatenate([rows, jnp.zeros((SEGS, 128 - RAYS), f32)], axis=1).T
    return jnp.concatenate([padded[:RAYS, s : s + 1] for s in range(SEGS)], axis=0)


def pack_kernel(own_ref, pos_ref, step_ref, cross_ref, send_ref, index_ref, dest_ref, data_ref):
    brick_col = column_of(cross_ref)
    step_col = column_of(step_ref)
    sub = iota((ENTRIES, ENTRIES), 0)
    lane = iota((ENTRIES, ENTRIES), 1)
    brick_row = jnp.sum(jnp.where(sub == lane, brick_col, 0.0), axis=0, keepdims=True)
    same = brick_col == brick_row
    rank_col = jnp.sum(jnp.where(same & (lane < sub), 1.0, 0.0), axis=1, keepdims=True)
    rank_row = jnp.sum(jnp.where(same & (sub < lane), 1.0, 0.0), axis=0, keepdims=True)
    own = own_ref[0]

    def place(number, rank):
        dest = jnp.floor(number * (1.0 / GROUP))
        member = (number - GROUP * dest).astype(jnp.int32) ^ own
        return dest, member.astype(f32) * CAP + rank

    dest_col, slot_col = place(brick_col, rank_col)
    dest_row, slot_row = place(brick_row, rank_row)
    pair_row = jnp.floor(slot_row * 0.5)
    half_row = slot_row - 2.0 * pair_row
    half_row = jnp.where(own_ref[1] < ROWS, half_row, 1.0 - half_row)
    target_row = pair_row * PEERS + dest_row
    here = sub.astype(f32) == target_row
    one_hot = jnp.concatenate(
        [jnp.where(here & (half_row == half), 1.0, 0.0).astype(bf16) for half in (0.0, 1.0)], axis=1
    )
    left = iota((RAYS, 128), 1) < SAMPLES
    for c in range(3):
        for q in range(SEGS // 2):
            x = pos_ref[c, :, 128 * q : 128 * q + 128]
            y = pltpu.roll(x, SAMPLES, 1)
            blocks = (
                (0, 2 * q, jnp.where(left, x, 0.0)),
                (0, 2 * q + 1, jnp.where(left, y, 0.0)),
                (1, 2 * q, jnp.where(left, 0.0, y)),
                (1, 2 * q + 1, jnp.where(left, 0.0, x)),
            )
            for half, s, block in blocks:
                row = half * ENTRIES + s * RAYS
                for part, value in enumerate(split3(block)):
                    data_ref[part, row : row + RAYS, 128 * c : 128 * c + 128] = value
    total = jnp.dot(one_hot, data_ref[2], preferred_element_type=f32)
    total += jnp.dot(one_hot, data_ref[1], preferred_element_type=f32)
    total += jnp.dot(one_hot, data_ref[0], preferred_element_type=f32)
    for pair in range(PAIRS):
        for c in range(3):
            send_ref[:, 3 * pair + c, :] = total[
                pair * PEERS : (pair + 1) * PEERS, 128 * c : 128 * c + 128
            ]
    to_dest = jnp.where(iota((PEERS, ENTRIES), 0).astype(f32) == dest_row, 1.0, 0.0)
    lane_128 = iota((ENTRIES, 128), 1)
    by_slot = jnp.where(lane_128.astype(f32) == slot_col, step_col, 0.0)
    send_ref[:, STEP_ROW, :] = pick(to_dest.astype(bf16), by_slot)
    send_ref[:, STEP_ROW + 1 :, :] = jnp.zeros((PEERS, WIRE - STEP_ROW - 1, 128), f32)
    index_ref[...] = jnp.where(lane_128 < 64, dest_col, slot_col)
    dest_ref[...] = jnp.broadcast_to(dest_row, (8, ENTRIES))


def pack(own, positions, spacing, crossings):
    vmem = pl.BlockSpec(memory_space=pltpu.VMEM)
    return pl.pallas_call(
        pack_kernel,
        out_shape=(
            jax.ShapeDtypeStruct((PEERS, WIRE, 128), f32),
            jax.ShapeDtypeStruct((ENTRIES, 128), f32),
            jax.ShapeDtypeStruct((8, ENTRIES), f32),
        ),
        in_specs=[pl.BlockSpec(memory_space=pltpu.SMEM), vmem, vmem, vmem],
        out_specs=(vmem, vmem, vmem),
        scratch_shapes=[pltpu.VMEM((3, 2 * ENTRIES, 384), bf16)],
        compiler_params=pltpu.CompilerParams(vmem_limit_bytes=VMEM),
        name="pack",
    )(own, positions, spacing, crossings)


def wave_constants():
    row = iota((64, 128), 0)
    k = row // 6
    within = row - 6 * k
    real = row < 6 * FREQS
    half_scale = jnp.where(real, 0.5, 0.0)
    for step in range(FREQS - 1):
        half_scale = jnp.where(k > step, half_scale * 2.0, half_scale)
    offset = jnp.where(real & (within >= 3), 0.0, 0.25)
    component = jnp.where(within >= 3, within - 3, within)
    component = component[:24]
    return half_scale, offset, component == 0, component == 1


def encode_into(enc_ref, recv_ref, slot, constants):
    half_scale, offset, first, second = constants
    pair = slot // 2
    near_side = (iota((8, 128), 1) < SAMPLES) == (slot == 2 * pair)
    for r in range(ROWS):
        p0, p1, p2 = [
            jnp.where(
                near_side,
                jnp.broadcast_to(recv_ref[r, pl.ds(3 * pair + c, 1), :], (8, 128)),
                jnp.broadcast_to(recv_ref[r + ROWS, pl.ds(3 * pair + c, 1), :], (8, 128)),
            )
            for c in range(3)
        ]
        p0, p1, p2 = [jnp.concatenate([p] * 3, axis=0) for p in (p0, p1, p2)]
        point = jnp.where(first, p0, jnp.where(second, p1, p2))
        point = jnp.concatenate([point, point, point[:16]], axis=0)
        turns = point * half_scale
        turns = turns - jnp.round(turns)
        y = 0.25 - jnp.abs(turns - offset)
        y = jnp.maximum(y, -0.5 - y)
        z = y * y
        value = SIN_TERMS[-1]
        for term in SIN_TERMS[-2::-1]:
            value = value * z + term
        enc_ref[:, 128 * r : 128 * r + 128] = (value * y).astype(bf16)


def spread(near, far, slot, lane_index):
    near_side = (iota((ROWS, 128), 1) < SAMPLES) == (slot % 2 == 0)
    return jnp.where(
        near_side, near[:, lane_index : lane_index + 1], far[:, lane_index : lane_index + 1]
    )


def same_half():
    i = iota((128, 128), 0)
    j = iota((128, 128), 1)
    return i, j, (i < SAMPLES) == (j < SAMPLES)


def as_matrix(mask):
    return jnp.where(mask, 1.0, 0.0)


def forward_kernel(*refs):
    recv_ref = refs[0]
    weight_refs = refs[1 : 1 + GROUP]
    small_ref, saved_ref, step_ref, used_ref = refs[1 + GROUP : 5 + GROUP]
    w_ref, head_ref, enc_ref, out_ref = refs[5 + GROUP :]

    for i in range(GROUP):
        packed = weight_refs[i][...]
        w_ref[i] = (0.5 * packed).T.astype(bf16)
        head_ref[i] = packed[48:64].astype(bf16)

    near = recv_ref[:ROWS, STEP_ROW, :]
    far = recv_ref[ROWS:, STEP_ROW, :]
    most = jnp.max(jnp.maximum(near, far), axis=0, keepdims=True)
    count = jnp.int32(0)
    for slot in range(SLOTS):
        if slot == SLOTS // 2:
            used_ref[SLOTS] = count
        used_ref[count] = slot
        count += (most[0, slot] > 0.0).astype(jnp.int32)
    used_ref[SLOTS + 1] = count
    for slot in range(SLOTS):
        step_ref[slot] = spread(near, far, slot, slot)
    out_ref[...] = jnp.zeros((4, SLOTS, ROWS, 128), f32)

    constants = wave_constants()

    def turn(number, carry):
        slot = used_ref[number]
        brick = slot // CAP
        encode_into(enc_ref, recv_ref, slot, constants)
        first = w_ref[brick]
        head = head_ref[brick]
        for n in range(TILE // FORWARD_CHUNK):
            half = jnp.dot(
                first, enc_ref[:, n * FORWARD_CHUNK : (n + 1) * FORWARD_CHUNK], preferred_element_type=f32
            )
            hidden = (half + half * jnp.tanh(half)).astype(bf16)
            output = jnp.dot(head, hidden, preferred_element_type=f32)
            for r in range(FORWARD_CHUNK // 128):
                row = n * (FORWARD_CHUNK // 128) + r
                for v in range(4):
                    out_ref[v, slot, row : row + 1, :] = output[
                        12 + v : 13 + v, 128 * r : 128 * r + 128
                    ]
        return carry

    lax.fori_loop(0, count, turn, 0)

    rows = SLOTS * ROWS
    i, j, same = same_half()
    until = as_matrix(same & (i <= j))
    outputs = [out_ref[v].reshape(rows, 128) for v in range(4)]
    steps = step_ref[...].reshape(rows, 128)
    raw = outputs[0]
    density = jnp.maximum(raw, 0.0) + jnp.log1p(jnp.exp(-jnp.abs(raw)))
    optical = density * steps
    inclusive = exact_dot(optical, until)
    leaving = jnp.exp(-inclusive)
    weight = jnp.exp(optical - inclusive) - leaving
    saved_ref[3] = jax.nn.sigmoid(raw).reshape(SLOTS, ROWS, 128)
    saved_ref[4] = weight.reshape(SLOTS, ROWS, 128)
    saved_ref[5] = leaving.reshape(SLOTS, ROWS, 128)
    total = as_matrix(((i < SAMPLES) & (j == 0)) | ((i >= SAMPLES) & (j == 1)))
    last = as_matrix(((i == SAMPLES - 1) & (j == 0)) | ((i == 127) & (j == 1)))
    results = []
    for v in range(3):
        colour = jax.nn.sigmoid(outputs[1 + v])
        saved_ref[v] = colour.reshape(SLOTS, ROWS, 128)
        results.append(exact_dot(weight * colour, total))
    results.append(exact_dot(leaving, last))
    lane = iota((ROWS, 128), 1)
    for side in range(2):
        gathered = jnp.zeros((ROWS, 128), f32)
        for v in range(4):
            for slot in range(SLOTS):
                half = (side + slot) % 2
                column = results[v][slot * ROWS : (slot + 1) * ROWS, half : half + 1]
                gathered = jnp.where(lane == v * SLOTS + slot, column, gathered)
        small_ref[side * ROWS : (side + 1) * ROWS, :] = gathered


def forward(received, weights):
    vmem = pl.BlockSpec(memory_space=pltpu.VMEM)
    return pl.pallas_call(
        forward_kernel,
        out_shape=(
            jax.ShapeDtypeStruct((PEERS, 128), f32),
            jax.ShapeDtypeStruct((6, SLOTS, ROWS, 128), f32),
            jax.ShapeDtypeStruct((SLOTS, ROWS, 128), f32),
            jax.ShapeDtypeStruct((SLOTS + 2,), jnp.int32),
        ),
        in_specs=[vmem] * (1 + GROUP),
        out_specs=(vmem, vmem, vmem, pl.BlockSpec(memory_space=pltpu.SMEM)),
        scratch_shapes=[
            pltpu.VMEM((GROUP, HIDDEN, 64), bf16),
            pltpu.VMEM((GROUP, 16, HIDDEN), bf16),
            pltpu.VMEM((64, TILE), bf16),
            pltpu.VMEM((4, SLOTS, ROWS, 128), f32),
        ],
        compiler_params=pltpu.CompilerParams(vmem_limit_bytes=VMEM),
        cost_estimate=matrix_cost(SLOTS * 2),
        name="forward",
    )(received, *weights)


def ray_kernel(small_ref, index_ref, dest_ref, target_ref, grads_ref, rendered_ref):
    lane = iota((ENTRIES, 128), 1)
    value = lane // SLOTS
    slot = (lane - value * SLOTS).astype(f32)
    dest_col = index_ref[:, 0:1]
    slot_col = index_ref[:, 64:65]
    to_entry = jnp.where(lane.astype(f32) == dest_col, 1.0, 0.0)
    small = jnp.concatenate([small_ref[...], jnp.zeros((128 - PEERS, 128), f32)], axis=0)
    mine = (slot == slot_col) & (value < 4)
    found = jnp.where(mine, exact_dot(to_entry, small), 0.0)
    i = iota((128, 128), 0)
    j = iota((128, 128), 1)
    segments = exact_dot(found, as_matrix((i // SLOTS == j) & (j < 4)))

    lane = iota((RAYS, 128), 1)
    parts = [segments[s * RAYS : (s + 1) * RAYS] for s in range(SEGS)]
    trans = [jnp.broadcast_to(part[:, 3:4], (RAYS, 128)) for part in parts]
    prefix = [jnp.ones((RAYS, 128), f32)]
    for s in range(SEGS - 1):
        prefix.append(prefix[s] * trans[s])
    rendered = prefix[0] * parts[0]
    for s in range(1, SEGS):
        rendered += prefix[s] * parts[s]
    residual = jnp.where(lane < 3, rendered - target_ref[...], 0.0)
    behind = jnp.zeros((RAYS, 128), f32)
    grads = [None] * SEGS
    for s in range(SEGS - 1, -1, -1):
        through = prefix[s] * jnp.sum(behind * residual, axis=1, keepdims=True)
        grads[s] = jnp.where(lane == 3, through, prefix[s] * residual)
        behind = parts[s] + trans[s] * behind
    spread_back = exact_dot(jnp.concatenate(grads, axis=0), as_matrix((j // SLOTS == i) & (i < 4)))
    to_dest = jnp.where(iota((PEERS, ENTRIES), 0).astype(f32) == dest_ref[0:1, :], 1.0, 0.0)
    grads_ref[...] = exact_dot(to_dest, jnp.where(mine, spread_back, 0.0))
    eye = as_matrix(iota((8, 128), 0) == iota((8, 128), 1))
    rendered_ref[...] = nt_dot(eye, rendered, lax.Precision.HIGHEST)[0:3]


def ray_level(small, index, dest, target):
    return pl.pallas_call(
        ray_kernel,
        out_shape=(
            jax.ShapeDtypeStruct((PEERS, 128), f32),
            jax.ShapeDtypeStruct((3, RAYS), f32),
        ),
        compiler_params=pltpu.CompilerParams(vmem_limit_bytes=VMEM),
        name="rays",
    )(small, index, dest, target)


def upstream_into(up_ref, grads_ref, saved_ref, step_ref):
    near = grads_ref[:ROWS]
    far = grads_ref[ROWS:]
    for v in range(4):
        for slot in range(SLOTS):
            up_ref[v, slot] = spread(near, far, slot, v * SLOTS + slot)

    rows = SLOTS * ROWS

    def flat(x):
        return x.reshape(rows, 128)

    i, j, same = same_half()
    beyond = as_matrix(same & (i > j))
    last = as_matrix(same & ((i == SAMPLES - 1) | (i == 127)))
    weight = flat(saved_ref[4])
    leaving = flat(saved_ref[5])
    shading = flat(saved_ref[0]) * flat(up_ref[0])
    shading += flat(saved_ref[1]) * flat(up_ref[1])
    shading += flat(saved_ref[2]) * flat(up_ref[2])
    after = exact_dot(weight * shading, beyond)
    grad_depth = shading * leaving - after - flat(up_ref[3]) * exact_dot(leaving, last)
    upstream = [grad_depth * flat(step_ref[...]) * flat(saved_ref[3])]
    for v in range(3):
        colour = flat(saved_ref[v])
        upstream.append(weight * flat(up_ref[v]) * colour * (1.0 - colour))
    for v in range(4):
        up_ref[v] = upstream[v].reshape(SLOTS, ROWS, 128)


def gradients(low, up_ref, recv_ref, used_ref, weight_refs, total_refs, scratch):
    w_ref, back_ref, enc_ref, row_ref = scratch
    for i, ref in enumerate(weight_refs):
        packed = 0.5 * ref[...]
        w_ref[i] = packed.T.astype(bf16)
        back_ref[i] = packed[48:64].T.astype(bf16)
    total_refs[...] = jnp.zeros(total_refs.shape, f32)
    row_ref[...] = jnp.zeros((16, TILE), f32)
    constants = wave_constants()

    def turn(number, carry):
        slot = used_ref[number]
        brick = slot // CAP - low
        encode_into(enc_ref, recv_ref, slot, constants)
        for v in range(4):
            rows_v = up_ref[v, slot]
            for r in range(ROWS):
                row_ref[12 + v : 13 + v, 128 * r : 128 * r + 128] = rows_v[r : r + 1, :]
        first = w_ref[brick]
        back = back_ref[brick]
        grad_first = jnp.zeros((64, HIDDEN), f32)
        grad_head = jnp.zeros((16, HIDDEN), f32)
        for n in range(TILE // BACKWARD_CHUNK):
            lanes = slice(n * BACKWARD_CHUNK, (n + 1) * BACKWARD_CHUNK)
            encoded = enc_ref[:, lanes]
            up = row_ref[:, lanes].astype(bf16)
            half = jnp.dot(first, encoded, preferred_element_type=f32)
            grad_hidden = jnp.dot(back, up, preferred_element_type=f32)
            bend = jnp.tanh(half)
            product = half * bend
            hidden = (half + product).astype(bf16)
            slope = (1.0 + bend) * ((1.0 + half) - product)
            grad_before = (grad_hidden * slope).astype(bf16)
            grad_first += nt_dot(encoded, grad_before)
            grad_head += nt_dot(up, hidden)
        total_refs[brick] += grad_first
        total_refs[brick, 48:64] += grad_head
        return carry

    if low:
        lax.fori_loop(used_ref[SLOTS], used_ref[SLOTS + 1], turn, 0)
    else:
        lax.fori_loop(0, used_ref[SLOTS], turn, 0)


HALF = GROUP // 2


def far_kernel(*refs):
    grads_ref, saved_ref, step_ref, recv_ref, used_ref = refs[:5]
    weight_refs = refs[5 : 5 + HALF]
    up_ref = refs[5 + HALF]
    total_refs = refs[6 + HALF : 6 + 2 * HALF]
    sum_ref = refs[6 + 2 * HALF]
    upstream_into(up_ref, grads_ref, saved_ref, step_ref)
    gradients(HALF, up_ref, recv_ref, used_ref, weight_refs, sum_ref, refs[7 + 2 * HALF :])
    for i in range(HALF):
        total_refs[i][...] = sum_ref[i]


def near_kernel(*refs):
    up_ref, recv_ref, used_ref = refs[:3]
    weight_refs = refs[3 : 3 + HALF]
    total_refs = refs[3 + HALF : 3 + 2 * HALF]
    sum_ref = refs[3 + 2 * HALF]
    gradients(0, up_ref, recv_ref, used_ref, weight_refs, sum_ref, refs[4 + 2 * HALF :])
    for i in range(HALF):
        total_refs[i][...] = sum_ref[i]


def backward_call(kernel, name, extra, operands, dense):
    vmem = pl.BlockSpec(memory_space=pltpu.VMEM)
    smem = pl.BlockSpec(memory_space=pltpu.SMEM)
    totals = tuple(jax.ShapeDtypeStruct((64, HIDDEN), f32) for _ in range(HALF))
    return pl.pallas_call(
        kernel,
        out_shape=extra + totals,
        in_specs=[vmem] * dense + [smem] + [vmem] * HALF,
        out_specs=tuple([vmem] * (len(extra) + HALF)),
        scratch_shapes=[
            pltpu.VMEM((HALF, 64, HIDDEN), f32),
            pltpu.VMEM((HALF, HIDDEN, 64), bf16),
            pltpu.VMEM((HALF, HIDDEN, 16), bf16),
            pltpu.VMEM((64, TILE), bf16),
            pltpu.VMEM((16, TILE), f32),
        ],
        compiler_params=pltpu.CompilerParams(vmem_limit_bytes=VMEM),
        cost_estimate=matrix_cost(SLOTS // 2 * 4),
        name=name,
    )(*operands)


def backward_far(grads, saved, steps, received, used, weights):
    dense = (jax.ShapeDtypeStruct((4, SLOTS, ROWS, 128), f32),)
    operands = (grads, saved, steps, received, used, *weights)
    return backward_call(far_kernel, "backward_far", dense, operands, 4)


def backward_near(upstream, received, used, weights):
    return backward_call(near_kernel, "backward_near", (), (upstream, received, used, *weights), 2)


def sum_kernel(*refs):
    total = refs[0][...]
    for ref in refs[1:GROUP]:
        total += ref[...]
    refs[GROUP][...] = total
    square = jnp.sum(jnp.sum(total * total, axis=1, keepdims=True), axis=0, keepdims=True)
    refs[GROUP + 1][...] = jnp.broadcast_to(square, refs[GROUP + 1].shape)


def add_up(partials, bricks):
    return pl.pallas_call(
        sum_kernel,
        out_shape=(
            jax.ShapeDtypeStruct((64, HIDDEN), f32),
            jax.ShapeDtypeStruct((bricks, 128), f32),
        ),
        name="add_up",
    )(*partials)


def normalize(total, squares, count):
    def body(total_ref, squares_ref, first_ref, head_ref):
        overall = jnp.sum(squares_ref[:, 0:1], axis=0, keepdims=True)
        scaled = total_ref[...] * lax.rsqrt(overall / count + NORM_EPS)
        first_ref[:, 0, :] = scaled[: 6 * FREQS]
        head_ref[0] = scaled[6 * FREQS :]

    first, head = pl.pallas_call(
        body,
        out_shape=(
            jax.ShapeDtypeStruct((6 * FREQS, 1, HIDDEN), f32),
            jax.ShapeDtypeStruct((1, 4, HIDDEN), f32),
        ),
        name="normalize",
    )(total, squares)
    return first.transpose(1, 2, 0), head


def with_member(x, difference):
    return lax.ppermute(x, "gz", [(i, i ^ difference) for i in range(GROUP)])


def exchange(x, axes):
    return lax.all_to_all(x, axes, split_axis=0, concat_axis=0, tiled=True)


def on_device(positions, spacing, crossings, target, first_weight, head_weight):
    own = jnp.concatenate(
        [first_weight[0].astype(f32).T, head_weight[0].astype(f32)], axis=0
    )
    weights = [own] + [with_member(own, difference) for difference in range(1, GROUP)]
    bricks = GROUP * PEERS
    own_place = jnp.stack([lax.axis_index("gz"), lax.axis_index(PEER_AXES)]).astype(jnp.int32)
    send, index, dest = pack(own_place, positions, spacing.T, crossings.T)
    target_rows = jnp.pad(target.T, ((0, 0), (0, 125)))
    received = exchange(send, PEER_AXES)
    small, saved, steps, used = forward(received, weights)
    grads, rendered = ray_level(exchange(small, PEER_AXES), index, dest, target_rows)
    grads = exchange(grads, PEER_AXES)
    upstream, *far = backward_far(grads, saved, steps, received, used, weights[HALF:])
    near = backward_near(upstream, received, used, weights[:HALF])
    arrived = [near[0]]
    arrived += [with_member(far[i], HALF + i) for i in range(HALF)]
    arrived += [with_member(near[i], i) for i in range(1, HALF)]
    total, square = add_up(arrived, bricks)
    squares = exchange(square, ALL)
    first_update, head_update = normalize(total, squares, bricks * (64 * HIDDEN))
    return (rendered, first_update, head_update)


def solution(mesh):
    in_specs = (
        P(None, ALL, None),
        P(ALL, None),
        P(ALL, None),
        P(None, ALL),
        P(ALL, None, None),
        P(ALL, None, None),
    )
    out_specs = (P(None, ALL), P(ALL, None, None), P(ALL, None, None))
    return jax.shard_map(
        on_device, mesh=mesh, in_specs=in_specs, out_specs=out_specs, check_vma=False
    )
```

time: 604 us -> 160 us (0.26)
  matrix products: 150 us -> 0 us
  other arithmetic: 139 us -> 0.6 us
  blocking collectives: 169 us -> 38.3 us
  local copies, waits for them, and re-layouts: 74 us -> 2.81 us
  Pallas kernels: 0 us -> 49.9 us
  starting transfers between devices: 20.2 us -> 45.1 us
  waiting for transfers between devices: 42.2 us -> 23.1 us
    dot_general x120 -> x0, matrix products: 150 us -> none  [the longest x24 65.6 us: network_grad(): lax.dot_general(grad_before, encoded, (((1,), (1,)), ((), ())), preferred...]
    another operation x147 -> x1, other arithmetic: 133 us -> 0.59 us  [on_device(): jnp.stack([lax.axis_index('gz'), lax.axis_index(PEER_AXES)])]
    psum x1 -> x0, blocking collectives: 74.3 us -> none  [on_device(): overall = lax.psum(square_sum, ('gx', 'gy', 'gz'))]
    all_to_all x3 -> x2, blocking collectives: 94.5 us -> 38.3 us  [exchange(): return lax.all_to_all(x, axes, split_axis=0, concat_axis=0, tiled=True)]
    pallas_call x0 -> x7, Pallas kernels: none -> 49.9 us  [the longest x2 24.3 us: backward_call(): pl.pallas_call(kernel, out_shape=extra + totals, in_specs=[vmem] * dense...]
    all_to_all x3 -> x2, waiting for transfers between devices: 42.2 us -> 13.4 us  [exchange(): return lax.all_to_all(x, axes, split_axis=0, concat_axis=0, tiled=True)]
    ppermute x0 -> x14, starting transfers between devices: none -> 24.4 us  [with_member(): return lax.ppermute(x, 'gz', [(i, i ^ difference) for i in range(GROUP)])]
    scatter x4 -> x0, local copies, waits for them, and re-layouts: 23.9 us -> none  [the longest x2 12 us: on_device(): jnp.zeros((4, total_slots, SAMPLES), jnp.float32).at[:, column, :]]
  transfers between devices with their start and end apart: 3 -> 16, of which waited for: 3 -> 9; matrix products, arithmetic and copies ran while one was open for 0% -> 0% of each run, Pallas kernels for 0% -> 0%
where the time goes in v1:
time: 160 us; the launch traced here: 161 us
  Pallas kernels  49.9 us (31%)
  starting transfers between devices  45.1 us (28%)
  blocking collectives  38.3 us (24%)
  waiting for transfers between devices  23.1 us (14%)
  local copies, waits for them, and re-layouts  2.81 us (2%)
    all_to_all x2, blocking collectives, exchange(): return lax.all_to_all(x, axes, split_axis=0, concat_axis=0, tiled=True)  38.3 us
    ppermute x14, starting transfers between devices, with_member(): return lax.ppermute(x, 'gz', [(i, i ^ difference) for i in range(GROUP)])  24.4 us
    pallas_call x2, Pallas kernels, backward_call(): pl.pallas_call(kernel, out_shape=extra + totals, in_specs=[vmem] * dense...  24.3 us
    all_to_all x2, starting transfers between devices, exchange(): return lax.all_to_all(x, axes, split_axis=0, concat_axis=0, tiled=True)  20.7 us
    pallas_call x1, Pallas kernels, forward(): pl.pallas_call(forward_kernel, out_shape=(jax.ShapeDtypeStruct((PEERS, 12...  15.1 us
    all_to_all x2, waiting for transfers between devices, exchange(): return lax.all_to_all(x, axes, split_axis=0, concat_axis=0, tiled=True)  13.4 us
    ppermute x14, waiting for transfers between devices, with_member(): return lax.ppermute(x, 'gz', [(i, i ^ difference) for i in range(GROUP)])  9.7 us
    pallas_call x1, Pallas kernels, pack(): pl.pallas_call(pack_kernel, out_shape=(jax.ShapeDtypeStruct((PEERS, WIRE,...  3.71 us
  transfers between devices with their start and end apart: 16, of which 9 were waited for; matrix products, arithmetic and copies ran while one was open for 0% of the time, Pallas kernels for 0%

profile of v1, /device:TPU:1, one launch (start us, length us, event | category | flops | bytes accessed | tf_op | source)
XLA Modules:
  0.0 160.6 jit_solution(15904422730976202315)
XLA Ops:
  0.7 0.6 pad_add_fusion.own_ref
  1.2 3.7 %pack.1 = (f32[32,40,128]{2,1,0:T(8,128)}, f32[384,128]{1,0:T(8,128)}, f32[8,384]{1,0:T(8,128)}) custom-call(s32[2]{0:T(128)} %pad_add_fusion.own_ref, f32[3,48,512]{2,1,0:T(8,128)} %pos_ref.1, f32[8,48]{1,0:T(8,128)} %bitcast.30, s32[8,48]{1,0:T(8,128)} %bitcast.31), custom_call_target="tpu_custom_call" | custom-call | tf_op jit(solution)/shard_map/pack/pallas_call | solution.py:143
  5.0 11.9 %all-to-all-start = ((f32[32,40,128]{2,1,0:T(8,128)}), f32[32,40,128]{2,1,0:T(8,128)S(1)}, u32[]{:S(2)}, u32[]{:S(2)}) async-start(f32[32,40,128]{2,1,0:T(8,128)} %get-tuple-element.25), calls=%async_computation | async-start | bytes 1310720 | tf_op jit(solution)/shard_map/all_to_all | solution.py:546
  16.9 3.7 %collective-permute-start.6 = (f32[64,256]{1,0:T(8,128)S(1)}, f32[64,256]{1,0:T(8,128)S(1)}, u32[]{:S(2)}, u32[]{:S(2)}) collective-permute-start(f32[64,256]{1,0:T(8,128)S(1)} %maximum_convert_fusion.refs_1_.refs_3_), channel_id=1, source_target_pairs={{0,7},{1,6},{2,5},{3,4},{4,3},{5,2},{6,1},{7,0},{8,15},{9,14},{10,... | collective-permute-start | bytes 196616 | tf_op jit(solution)/shard_map/ppermute | solution.py:542
  20.6 1.4 collective-permute-start.4
  21.9 2.0 %collective-permute-start.3 = (f32[64,256]{1,0:T(8,128)S(1)}, f32[64,256]{1,0:T(8,128)S(1)}, u32[]{:S(2)}, u32[]{:S(2)}) collective-permute-start(f32[64,256]{1,0:T(8,128)S(1)} %maximum_convert_fusion.refs_1_.refs_3_), channel_id=1, source_target_pairs={{0,4},{1,5},{2,6},{3,7},{4,0},{5,1},{6,2},{7,3},{8,12},{9,13},{10,... | collective-permute-start | bytes 196616 | tf_op jit(solution)/shard_map/ppermute | solution.py:542
  24.1 1.4 collective-permute-start.1
  25.6 3.1 %collective-permute-done.5.refs_7_ = f32[64,256]{1,0:T(8,128)S(1)} collective-permute-done((f32[64,256]{1,0:T(8,128)S(1)}, f32[64,256]{1,0:T(8,128)S(1)}, u32[]{:S(2)}, u32[]{:S(2)}) %collective-permute-start.5) | collective-permute-done | bytes 65568 | tf_op jit(solution)/shard_map/ppermute | solution.py:542
  29.1 0.6 collective-permute-done.2.refs_4_.refs_6_
  30.0 5.5 %all-to-all-done.refs_0_.refs_3_.refs_1_ = f32[32,40,128]{2,1,0:T(8,128)S(1)} async-done(((f32[32,40,128]{2,1,0:T(8,128)}), f32[32,40,128]{2,1,0:T(8,128)S(1)}, u32[]{:S(2)}, u32[]{:S(2)}) %all-to-all-start) | async-done | bytes 655392 | tf_op jit(solution)/shard_map/all_to_all | solution.py:546
  35.6 0.8 copy-done
  36.4 15.1 %forward.1 = (f32[32,128]{1,0:T(8,128)}, f32[6,24,16,128]{3,2,1,0:T(8,128)}, f32[24,16,128]{2,1,0:T(8,128)}, s32[26]{0:T(128)}) custom-call(f32[32,40,128]{2,1,0:T(8,128)} %copy-done, f32[64,256]{1,0:T(8,128)} %copy-done.1, f32[64,256]{1,0:T(8,128)} %copy-done.19, f32[64,256]{1,0:T(8,128)} %copy-done.17, f32[64,256]{1,0:T(8,128)} %copy-done.14, ...), custom_call_target="tpu_custom_call" | custom-call | flops 12884901888 | bytes 4194304 | tf_op jit(solution)/shard_map/forward/pallas_call | solution.py:300
  51.5 8.8 %all-to-all-start.1 = ((f32[32,1,128]{2,1,0:T(1,128)}), f32[32,1,128]{2,1,0:T(1,128)S(1)}, u32[]{:S(2)}, u32[]{:S(2)}) async-start(f32[32,1,128]{2,1,0:T(1,128)} %bitcast.28), calls=%async_computation.1 | async-start | bytes 32768 | tf_op jit(solution)/shard_map/all_to_all | solution.py:546
  60.4 0.6 pad.4.target_ref
  61.0 7.9 %all-to-all-done.1 = f32[32,1,128]{2,1,0:T(1,128)S(1)} async-done(((f32[32,1,128]{2,1,0:T(1,128)}), f32[32,1,128]{2,1,0:T(1,128)S(1)}, u32[]{:S(2)}, u32[]{:S(2)}) %all-to-all-start.1) | async-done | bytes 16416 | tf_op jit(solution)/shard_map/all_to_all | solution.py:546
  68.9 0.6 copy-done.9
  69.5 3.3 %rays.1 = (f32[32,128]{1,0:T(8,128)}, f32[3,48]{1,0:T(4,128)}) custom-call(f32[32,128]{1,0:T(8,128)} %bitcast.25, f32[384,128]{1,0:T(8,128)} %get-tuple-element.27.index_ref, f32[8,384]{1,0:T(8,128)} %get-tuple-element.28.dest_ref, f32[48,128]{1,0:T(8,128)} %pad.4.target_ref), custom_call_target="tpu_custom_call" | custom-call | tf_op jit(solution)/shard_map/rays/pallas_call | solution.py:360
  72.8 13.1 %all_to_all.38 = f32[32,1,128]{2,1,0:T(1,128)} all-to-all(f32[32,1,128]{2,1,0:T(1,128)} %bitcast.29), channel_id=1, replica_groups=mesh['gx'=8,'gy'=4,'gz'=8] {'gx','gy'}, dimensions={0} | all-to-all | bytes 32768 | tf_op jit(solution)/shard_map/all_to_all | solution.py:546
  86.0 11.8 %backward_far.1 = (f32[4,24,16,128]{3,2,1,0:T(8,128)}, f32[64,256]{1,0:T(8,128)}, f32[64,256]{1,0:T(8,128)}, f32[64,256]{1,0:T(8,128)}, f32[64,256]{1,0:T(8,128)}) custom-call(f32[32,128]{1,0:T(8,128)} %bitcast.27, f32[6,24,16,128]{3,2,1,0:T(8,128)} %get-tuple-element.31.refs_1_, f32[24,16,128]{2,1,0:T(8,128)} %get-tuple-element.32.refs_2_, ...), custom_call_target="tpu_custom_call" | custom-call | flops 12884901888 | bytes 4194304 | tf_op jit(solution)/shard_map/backward_far/pallas_call | solution.py:475
  97.8 12.4 %backward_near.1 = (f32[64,256]{1,0:T(8,128)}, f32[64,256]{1,0:T(8,128)}, f32[64,256]{1,0:T(8,128)}, f32[64,256]{1,0:T(8,128)}) custom-call(f32[4,24,16,128]{3,2,1,0:T(8,128)} %get-tuple-element.34.refs_0_, f32[32,40,128]{2,1,0:T(8,128)} %copy-done, s32[26]{0:T(128)} %get-tuple-element.33.refs_4_.refs_2_, f32[64,256]{1,0:T(8,128)} %copy-done.1, ...), custom_call_target="tpu_custom_call" | custom-call | flops 12884901888 | bytes 4194304 | tf_op jit(solution)/shard_map/backward_near/pallas_call | solution.py:475
  110.2 4.2 %collective-permute-start.11 = (f32[64,256]{1,0:T(8,128)}, f32[64,256]{1,0:T(8,128)S(1)}, u32[]{:S(2)}, u32[]{:S(2)}) collective-permute-start(f32[64,256]{1,0:T(8,128)} %get-tuple-element.40), channel_id=1, source_target_pairs={{0,1},{1,0},{2,3},{3,2},{4,5},{5,4},{6,7},{7,6},{8,9},{9,8},{10,11... | collective-permute-start | bytes 196616 | tf_op jit(solution)/shard_map/ppermute | solution.py:542
  114.5 1.9 %collective-permute-start.12 = (f32[64,256]{1,0:T(8,128)}, f32[64,256]{1,0:T(8,128)S(1)}, u32[]{:S(2)}, u32[]{:S(2)}) collective-permute-start(f32[64,256]{1,0:T(8,128)} %get-tuple-element.41), channel_id=1, source_target_pairs={{0,2},{1,3},{2,0},{3,1},{4,6},{5,7},{6,4},{7,5},{8,10},{9,11},{10,... | collective-permute-start | bytes 196616 | tf_op jit(solution)/shard_map/ppermute | solution.py:542
  116.5 5.6 %collective-permute-start.7 = (f32[64,256]{1,0:T(8,128)S(1)}, f32[64,256]{1,0:T(8,128)S(1)}, u32[]{:S(2)}, u32[]{:S(2)}) collective-permute-start(f32[64,256]{1,0:T(8,128)S(1)} %copy-done.23), channel_id=1, source_target_pairs={{0,4},{1,5},{2,6},{3,7},{4,0},{5,1},{6,2},{7,3},{8,12},{9,13},{10,... | collective-permute-start | bytes 196616 | tf_op jit(solution)/shard_map/ppermute | solution.py:542
  122.2 3.1 %collective-permute-start.9 = (f32[64,256]{1,0:T(8,128)S(1)}, f32[64,256]{1,0:T(8,128)S(1)}, u32[]{:S(2)}, u32[]{:S(2)}) collective-permute-start(f32[64,256]{1,0:T(8,128)S(1)} %copy-done.21), channel_id=1, source_target_pairs={{0,6},{1,7},{2,4},{3,5},{4,2},{5,3},{6,0},{7,1},{8,14},{9,15},{10,... | collective-permute-start | bytes 196616 | tf_op jit(solution)/shard_map/ppermute | solution.py:542
  125.6 1.1 collective-permute-done.7.refs_1_
  126.7 1.7 %collective-permute-done.8.refs_2_ = f32[64,256]{1,0:T(8,128)S(1)} collective-permute-done((f32[64,256]{1,0:T(8,128)S(1)}, f32[64,256]{1,0:T(8,128)S(1)}, u32[]{:S(2)}, u32[]{:S(2)}) %collective-permute-start.8) | collective-permute-done | bytes 65568 | tf_op jit(solution)/shard_map/ppermute | solution.py:542
  128.3 1.6 collective-permute-done.9.refs_3_
  129.9 1.4 collective-permute-done.10.refs_4_
  131.3 0.6 copy-done.8
  131.9 1.8 %add_up.1 = (f32[64,256]{1,0:T(8,128)}, f32[256,128]{1,0:T(8,128)}) custom-call(f32[64,256]{1,0:T(8,128)} %get-tuple-element.35.refs_0_, f32[64,256]{1,0:T(8,128)} %copy-done.5, f32[64,256]{1,0:T(8,128)} %copy-done.6, f32[64,256]{1,0:T(8,128)} %copy-done.7, f32[64,256]{1,0:T(8,128)} %copy-done.8, f32[64,256]{1,0:T(8,128)} %copy-done.2, f32[64,256]{1,0:T(8,128)} %copy-done.3, ...), custom_call_target="tpu_custom_call" | custom-call | tf_op jit(solution)/shard_map/add_up/pallas_call | solution.py:513
  133.8 25.2 %all_to_all.39 = f32[256,1,128]{2,1,0:T(1,128)} all-to-all(f32[256,1,128]{2,1,0:T(1,128)} %bitcast.23), channel_id=1, replica_groups=mesh['gx'=8,'gy'=4,'gz'=8] {'gx','gy','gz'}, dimensions={0} | all-to-all | bytes 262144 | tf_op jit(solution)/shard_map/all_to_all | solution.py:546
  158.9 1.7 %normalize.1 = (f32[60,1,256]{2,1,0:T(1,128)}, f32[1,4,256]{2,1,0:T(4,128)}) custom-call(f32[64,256]{1,0:T(8,128)} %get-tuple-element.43.total_ref, f32[256,128]{1,0:T(8,128)} %bitcast.22), custom_call_target="tpu_custom_call" | custom-call | tf_op jit(solution)/shard_map/normalize/pallas_call | solution.py:530
  (61 shorter events, 1.6 us)
Async XLA Ops:
  0.6 16.2 %copy-start.11 = (bf16[1,4,256]{2,1,0:T(4,128)(2,1)S(1)}, bf16[1,4,256]{2,1,0:T(4,128)(2,1)}, u32[]{:S(2)}) copy-start(bf16[1,4,256]{2,1,0:T(4,128)(2,1)} %param.11) | copy-start | bytes 6148
  0.6 16.2 %copy-start.10 = (bf16[1,256,60]{1,2,0:T(8,128)(2,1)S(1)}, bf16[1,256,60]{1,2,0:T(8,128)(2,1)}, u32[]{:S(2)}) copy-start(bf16[1,256,60]{1,2,0:T(8,128)(2,1)} %param.10) | copy-start | bytes 92164
  5.0 30.6 %all-to-all-start = ((f32[32,40,128]{2,1,0:T(8,128)}), f32[32,40,128]{2,1,0:T(8,128)S(1)}, u32[]{:S(2)}, u32[]{:S(2)}) async-start(f32[32,40,128]{2,1,0:T(8,128)} %get-tuple-element.25), calls=%async_computation | async-start | bytes 1310720 | tf_op jit(solution)/shard_map/all_to_all | solution.py:546
  16.9 18.7 %copy-start.1 = (f32[64,256]{1,0:T(8,128)}, f32[64,256]{1,0:T(8,128)S(1)}, u32[]{:S(2)}) copy-start(f32[64,256]{1,0:T(8,128)S(1)} %maximum_convert_fusion.refs_1_.refs_3_) | copy-start | bytes 196612
  16.9 43.4 %copy-start.12 = (f32[3,48]{1,0:T(4,128)S(1)}, f32[3,48]{1,0:T(4,128)}, u32[]{:S(2)}) copy-start(f32[3,48]{1,0:T(4,128)} %param.9) | copy-start | bytes 1732
  16.9 7.3 %collective-permute-start.6 = (f32[64,256]{1,0:T(8,128)S(1)}, f32[64,256]{1,0:T(8,128)S(1)}, u32[]{:S(2)}, u32[]{:S(2)}) collective-permute-start(f32[64,256]{1,0:T(8,128)S(1)} %maximum_convert_fusion.refs_1_.refs_3_), channel_id=1, source_target_pairs={{0,7},{1,6},{2,5},{3,4},{4,3},{5,2},{6,1},{7,0},{8,15},{9,14},{10,... | collective-permute-start | bytes 196616 | tf_op jit(solution)/shard_map/ppermute | solution.py:542
  20.5 8.1 %collective-permute-start.5 = (f32[64,256]{1,0:T(8,128)S(1)}, f32[64,256]{1,0:T(8,128)S(1)}, u32[]{:S(2)}, u32[]{:S(2)}) collective-permute-start(f32[64,256]{1,0:T(8,128)S(1)} %maximum_convert_fusion.refs_1_.refs_3_), channel_id=1, source_target_pairs={{0,6},{1,7},{2,4},{3,5},{4,2},{5,3},{6,0},{7,1},{8,14},{9,15},{10,... | collective-permute-start | bytes 196616 | tf_op jit(solution)/shard_map/ppermute | solution.py:542
  20.6 8.5 %collective-permute-start.4 = (f32[64,256]{1,0:T(8,128)S(1)}, f32[64,256]{1,0:T(8,128)S(1)}, u32[]{:S(2)}, u32[]{:S(2)}) collective-permute-start(f32[64,256]{1,0:T(8,128)S(1)} %maximum_convert_fusion.refs_1_.refs_3_), channel_id=1, source_target_pairs={{0,5},{1,4},{2,7},{3,6},{4,1},{5,0},{6,3},{7,2},{8,13},{9,12},{10,... | collective-permute-start | bytes 196616 | tf_op jit(solution)/shard_map/ppermute | solution.py:542
  21.9 7.2 %collective-permute-start.3 = (f32[64,256]{1,0:T(8,128)S(1)}, f32[64,256]{1,0:T(8,128)S(1)}, u32[]{:S(2)}, u32[]{:S(2)}) collective-permute-start(f32[64,256]{1,0:T(8,128)S(1)} %maximum_convert_fusion.refs_1_.refs_3_), channel_id=1, source_target_pairs={{0,4},{1,5},{2,6},{3,7},{4,0},{5,1},{6,2},{7,3},{8,12},{9,13},{10,... | collective-permute-start | bytes 196616 | tf_op jit(solution)/shard_map/ppermute | solution.py:542
  23.9 5.8 %collective-permute-start.2 = (f32[64,256]{1,0:T(8,128)S(1)}, f32[64,256]{1,0:T(8,128)S(1)}, u32[]{:S(2)}, u32[]{:S(2)}) collective-permute-start(f32[64,256]{1,0:T(8,128)S(1)} %maximum_convert_fusion.refs_1_.refs_3_), channel_id=1, source_target_pairs={{0,3},{1,2},{2,1},{3,0},{4,7},{5,6},{6,5},{7,4},{8,11},{9,10},{10,... | collective-permute-start | bytes 196616 | tf_op jit(solution)/shard_map/ppermute | solution.py:542
  24.1 11.4 %copy-start.13 = (f32[64,256]{1,0:T(8,128)}, f32[64,256]{1,0:T(8,128)S(1)}, u32[]{:S(2)}) copy-start(f32[64,256]{1,0:T(8,128)S(1)} %collective-permute-done.6.refs_8_) | copy-start | bytes 196612
  24.1 5.5 %collective-permute-start.1 = (f32[64,256]{1,0:T(8,128)S(1)}, f32[64,256]{1,0:T(8,128)S(1)}, u32[]{:S(2)}, u32[]{:S(2)}) collective-permute-start(f32[64,256]{1,0:T(8,128)S(1)} %maximum_convert_fusion.refs_1_.refs_3_), channel_id=1, source_target_pairs={{0,2},{1,3},{2,0},{3,1},{4,6},{5,7},{6,4},{7,5},{8,10},{9,11},{10,... | collective-permute-start | bytes 196616 | tf_op jit(solution)/shard_map/ppermute | solution.py:542
  28.7 6.9 %copy-start.15 = (f32[64,256]{1,0:T(8,128)}, f32[64,256]{1,0:T(8,128)S(1)}, u32[]{:S(2)}) copy-start(f32[64,256]{1,0:T(8,128)S(1)} %collective-permute-done.5.refs_7_) | copy-start | bytes 196612
  28.7 1.3 collective-permute-start
  29.1 6.5 %copy-start.16 = (f32[64,256]{1,0:T(8,128)}, f32[64,256]{1,0:T(8,128)S(1)}, u32[]{:S(2)}) copy-start(f32[64,256]{1,0:T(8,128)S(1)} %collective-permute-done.4.refs_6_) | copy-start | bytes 196612
  29.1 6.5 %copy-start.18 = (f32[64,256]{1,0:T(8,128)}, f32[64,256]{1,0:T(8,128)S(1)}, u32[]{:S(2)}) copy-start(f32[64,256]{1,0:T(8,128)S(1)} %collective-permute-done.3.refs_5_) | copy-start | bytes 196612
  29.7 5.9 %copy-start.14 = (f32[64,256]{1,0:T(8,128)}, f32[64,256]{1,0:T(8,128)S(1)}, u32[]{:S(2)}) copy-start(f32[64,256]{1,0:T(8,128)S(1)} %collective-permute-done.2.refs_4_.refs_6_) | copy-start | bytes 196612
  29.7 5.9 %copy-start.17 = (f32[64,256]{1,0:T(8,128)}, f32[64,256]{1,0:T(8,128)S(1)}, u32[]{:S(2)}) copy-start(f32[64,256]{1,0:T(8,128)S(1)} %collective-permute-done.1.refs_3_.refs_5_) | copy-start | bytes 196612
  51.5 17.4 %all-to-all-start.1 = ((f32[32,1,128]{2,1,0:T(1,128)}), f32[32,1,128]{2,1,0:T(1,128)S(1)}, u32[]{:S(2)}, u32[]{:S(2)}) async-start(f32[32,1,128]{2,1,0:T(1,128)} %bitcast.28), calls=%async_computation.1 | async-start | bytes 32768 | tf_op jit(solution)/shard_map/all_to_all | solution.py:546
  97.8 18.7 %copy-start.23 = (f32[64,256]{1,0:T(8,128)S(1)}, f32[64,256]{1,0:T(8,128)}, u32[]{:S(2)}) copy-start(f32[64,256]{1,0:T(8,128)} %get-tuple-element.36) | copy-start | bytes 196612
  97.8 24.3 %copy-start.22 = (f32[64,256]{1,0:T(8,128)S(1)}, f32[64,256]{1,0:T(8,128)}, u32[]{:S(2)}) copy-start(f32[64,256]{1,0:T(8,128)} %get-tuple-element.37) | copy-start | bytes 196612
  97.8 24.4 %copy-start.21 = (f32[64,256]{1,0:T(8,128)S(1)}, f32[64,256]{1,0:T(8,128)}, u32[]{:S(2)}) copy-start(f32[64,256]{1,0:T(8,128)} %get-tuple-element.38) | copy-start | bytes 196612
  97.8 27.6 %copy-start.20 = (f32[64,256]{1,0:T(8,128)S(1)}, f32[64,256]{1,0:T(8,128)}, u32[]{:S(2)}) copy-start(f32[64,256]{1,0:T(8,128)} %get-tuple-element.39) | copy-start | bytes 196612
  110.2 12.0 %collective-permute-start.11 = (f32[64,256]{1,0:T(8,128)}, f32[64,256]{1,0:T(8,128)S(1)}, u32[]{:S(2)}, u32[]{:S(2)}) collective-permute-start(f32[64,256]{1,0:T(8,128)} %get-tuple-element.40), channel_id=1, source_target_pairs={{0,1},{1,0},{2,3},{3,2},{4,5},{5,4},{6,7},{7,6},{8,9},{9,8},{10,11... | collective-permute-start | bytes 196616 | tf_op jit(solution)/shard_map/ppermute | solution.py:542
  114.5 10.9 %collective-permute-start.12 = (f32[64,256]{1,0:T(8,128)}, f32[64,256]{1,0:T(8,128)S(1)}, u32[]{:S(2)}, u32[]{:S(2)}) collective-permute-start(f32[64,256]{1,0:T(8,128)} %get-tuple-element.41), channel_id=1, source_target_pairs={{0,2},{1,3},{2,0},{3,1},{4,6},{5,7},{6,4},{7,5},{8,10},{9,11},{10,... | collective-permute-start | bytes 196616 | tf_op jit(solution)/shard_map/ppermute | solution.py:542
  116.4 9.2 %collective-permute-start.13 = (f32[64,256]{1,0:T(8,128)}, f32[64,256]{1,0:T(8,128)S(1)}, u32[]{:S(2)}, u32[]{:S(2)}) collective-permute-start(f32[64,256]{1,0:T(8,128)} %get-tuple-element.42), channel_id=1, source_target_pairs={{0,3},{1,2},{2,1},{3,0},{4,7},{5,6},{6,5},{7,4},{8,11},{9,10},{10,... | collective-permute-start | bytes 196616 | tf_op jit(solution)/shard_map/ppermute | solution.py:542
  116.5 10.1 %collective-permute-start.7 = (f32[64,256]{1,0:T(8,128)S(1)}, f32[64,256]{1,0:T(8,128)S(1)}, u32[]{:S(2)}, u32[]{:S(2)}) collective-permute-start(f32[64,256]{1,0:T(8,128)S(1)} %copy-done.23), channel_id=1, source_target_pairs={{0,4},{1,5},{2,6},{3,7},{4,0},{5,1},{6,2},{7,3},{8,12},{9,13},{10,... | collective-permute-start | bytes 196616 | tf_op jit(solution)/shard_map/ppermute | solution.py:542
  122.1 6.3 %collective-permute-start.8 = (f32[64,256]{1,0:T(8,128)S(1)}, f32[64,256]{1,0:T(8,128)S(1)}, u32[]{:S(2)}, u32[]{:S(2)}) collective-permute-start(f32[64,256]{1,0:T(8,128)S(1)} %copy-done.22), channel_id=1, source_target_pairs={{0,5},{1,4},{2,7},{3,6},{4,1},{5,0},{6,3},{7,2},{8,13},{9,12},{10,... | collective-permute-start | bytes 196616 | tf_op jit(solution)/shard_map/ppermute | solution.py:542
  122.2 9.1 %copy-start.2 = (f32[64,256]{1,0:T(8,128)}, f32[64,256]{1,0:T(8,128)S(1)}, u32[]{:S(2)}) copy-start(f32[64,256]{1,0:T(8,128)S(1)} %collective-permute-done.11.refs_5_) | copy-start | bytes 196612
  122.2 7.7 %collective-permute-start.9 = (f32[64,256]{1,0:T(8,128)S(1)}, f32[64,256]{1,0:T(8,128)S(1)}, u32[]{:S(2)}, u32[]{:S(2)}) collective-permute-start(f32[64,256]{1,0:T(8,128)S(1)} %copy-done.21), channel_id=1, source_target_pairs={{0,6},{1,7},{2,4},{3,5},{4,2},{5,3},{6,0},{7,1},{8,14},{9,15},{10,... | collective-permute-start | bytes 196616 | tf_op jit(solution)/shard_map/ppermute | solution.py:542
  125.4 5.9 %copy-start.3 = (f32[64,256]{1,0:T(8,128)}, f32[64,256]{1,0:T(8,128)S(1)}, u32[]{:S(2)}) copy-start(f32[64,256]{1,0:T(8,128)S(1)} %collective-permute-done.12.refs_6_) | copy-start | bytes 196612
  125.4 5.9 %collective-permute-start.10 = (f32[64,256]{1,0:T(8,128)S(1)}, f32[64,256]{1,0:T(8,128)S(1)}, u32[]{:S(2)}, u32[]{:S(2)}) collective-permute-start(f32[64,256]{1,0:T(8,128)S(1)} %copy-done.20), channel_id=1, source_target_pairs={{0,7},{1,6},{2,5},{3,4},{4,3},{5,2},{6,1},{7,0},{8,15},{9,14},{10,... | collective-permute-start | bytes 196616 | tf_op jit(solution)/shard_map/ppermute | solution.py:542
  (8 other events, 22.5 us)

commit v2 on v1

v2 whole, which is shorter than its diff:
```python
import jax
import jax.numpy as jnp
from jax import lax
from jax.experimental import pallas as pl
from jax.experimental.pallas import tpu as pltpu
from jax.sharding import PartitionSpec as P

FREQS = 10
SAMPLES = 64
SEGS = 8
CAP = 3
ANCHOR = 5
NORM_EPS = 1e-06

RAYS = 48
GROUP = 8
PEERS = 32
SLOTS = GROUP * CAP
PAIRS = SLOTS // 2
ROWS = PEERS // 2
PITCH = ROWS + 1
TILE = PEERS * SAMPLES
ENTRIES = RAYS * SEGS
LIST = SLOTS + 2
STEP_ROW = 3 * PAIRS
WIRE = STEP_ROW + 1
HIDDEN = 256
FORWARD_CHUNK = 2048
BACKWARD_CHUNK = 512
VMEM = 56 * 1024 * 1024
SOME_VMEM = 24 * 1024 * 1024
ALL = ("gx", "gy", "gz")
PEER_AXES = ("gx", "gy")
GROUP_AXIS = "gz"

SIN_TERMS = (
    6.283185160116253,
    -41.34165503574907,
    81.60100428250003,
    -76.54978619700827,
    39.536730859838705,
)

f32 = jnp.float32
bf16 = jnp.bfloat16


def iota(shape, dim):
    return lax.broadcasted_iota(jnp.int32, shape, dim)


def nt_dot(a, b, precision=None):
    return lax.dot_general(
        a, b, (((1,), (1,)), ((), ())), preferred_element_type=f32, precision=precision
    )


def tn_dot(a, b):
    return lax.dot_general(a, b, (((0,), (0,)), ((), ())), preferred_element_type=f32)


def matrix_cost(tile_passes):
    return pl.CostEstimate(
        flops=tile_passes * 2 * HIDDEN * HIDDEN * TILE, bytes_accessed=4 << 20, transcendentals=0
    )


def wire_row(row):
    return pl.ds(128 * row if isinstance(row, int) else pl.multiple_of(128 * row, 128), 128)


def split3(x):
    high = x.astype(bf16)
    rest = x - high.astype(f32)
    mid = rest.astype(bf16)
    return high, mid, (rest - mid.astype(f32)).astype(bf16)


def pick(one_hot, x):
    high, mid, low = split3(x)
    total = jnp.dot(one_hot, low, preferred_element_type=f32)
    total += jnp.dot(one_hot, mid, preferred_element_type=f32)
    return total + jnp.dot(one_hot, high, preferred_element_type=f32)


def add_lanes(x, mask):
    ones = as_matrix(mask).astype(bf16)
    high, mid, low = split3(x)
    total = jnp.dot(low, ones, preferred_element_type=f32)
    total += jnp.dot(mid, ones, preferred_element_type=f32)
    return total + jnp.dot(high, ones, preferred_element_type=f32)


def column_of(rows_ref):
    rows = rows_ref[...].astype(f32)
    padded = jnp.concatenate([rows, jnp.zeros((SEGS, 128 - RAYS), f32)], axis=1).T
    return jnp.concatenate([padded[:RAYS, s : s + 1] for s in range(SEGS)], axis=0)


def pack_kernel(
    member_ref, peer_ref, pos_ref, step_ref, cross_ref, send_ref, index_ref, dest_ref, data_ref
):
    brick_col = column_of(cross_ref)
    step_col = column_of(step_ref)
    sub = iota((ENTRIES, ENTRIES), 0)
    lane = iota((ENTRIES, ENTRIES), 1)
    brick_row = jnp.sum(jnp.where(sub == lane, brick_col, 0.0), axis=0, keepdims=True)
    same = brick_col == brick_row
    rank_col = jnp.sum(jnp.where(same & (lane < sub), 1.0, 0.0), axis=1, keepdims=True)
    rank_row = jnp.sum(jnp.where(same & (sub < lane), 1.0, 0.0), axis=0, keepdims=True)
    own = member_ref[0].astype(f32)

    def place(number, rank):
        dest = jnp.floor(number * (1.0 / GROUP))
        ahead = number - GROUP * dest - own
        ahead = jnp.where(ahead < 0.0, ahead + GROUP, ahead)
        return dest, ahead * CAP + rank

    dest_col, slot_col = place(brick_col, rank_col)
    dest_row, slot_row = place(brick_row, rank_row)
    pair_row = jnp.floor(slot_row * 0.5)
    half_row = slot_row - 2.0 * pair_row
    half_row = jnp.where(peer_ref[0] < ROWS, half_row, 1.0 - half_row)
    target_row = pair_row * PEERS + dest_row
    here = sub.astype(f32) == target_row
    one_hot = jnp.concatenate(
        [jnp.where(here & (half_row == half), 1.0, 0.0).astype(bf16) for half in (0.0, 1.0)], axis=1
    )
    left = iota((RAYS, 128), 1) < SAMPLES
    for c in range(3):
        for q in range(SEGS // 2):
            x = pos_ref[c, :, 128 * q : 128 * q + 128]
            y = pltpu.roll(x, SAMPLES, 1)
            blocks = (
                (0, 2 * q, jnp.where(left, x, 0.0)),
                (0, 2 * q + 1, jnp.where(left, y, 0.0)),
                (1, 2 * q, jnp.where(left, 0.0, y)),
                (1, 2 * q + 1, jnp.where(left, 0.0, x)),
            )
            for half, s, block in blocks:
                row = half * ENTRIES + s * RAYS
                for part, value in enumerate(split3(block)):
                    data_ref[part, row : row + RAYS, 128 * c : 128 * c + 128] = value
    total = jnp.dot(one_hot, data_ref[2], preferred_element_type=f32)
    total += jnp.dot(one_hot, data_ref[1], preferred_element_type=f32)
    total += jnp.dot(one_hot, data_ref[0], preferred_element_type=f32)
    for pair in range(PAIRS):
        for c in range(3):
            send_ref[:, 0, wire_row(3 * pair + c)] = total[
                pair * PEERS : (pair + 1) * PEERS, 128 * c : 128 * c + 128
            ]
    to_dest = jnp.where(iota((PEERS, ENTRIES), 0).astype(f32) == dest_row, 1.0, 0.0)
    lane_128 = iota((ENTRIES, 128), 1)
    by_slot = jnp.where(lane_128.astype(f32) == slot_col, step_col, 0.0)
    send_ref[:, 0, wire_row(STEP_ROW)] = pick(to_dest.astype(bf16), by_slot)
    index_ref[...] = jnp.where(lane_128 < 64, dest_col, slot_col)
    dest_ref[...] = jnp.broadcast_to(dest_row, (8, ENTRIES))


def pack(member, peer, positions, spacing, crossings):
    vmem = pl.BlockSpec(memory_space=pltpu.VMEM)
    smem = pl.BlockSpec(memory_space=pltpu.SMEM)
    return pl.pallas_call(
        pack_kernel,
        out_shape=(
            jax.ShapeDtypeStruct((PEERS, 1, 128 * WIRE), f32),
            jax.ShapeDtypeStruct((ENTRIES, 128), f32),
            jax.ShapeDtypeStruct((8, ENTRIES), f32),
        ),
        in_specs=[smem, smem, vmem, vmem, vmem],
        out_specs=(vmem, vmem, vmem),
        scratch_shapes=[pltpu.VMEM((3, 2 * ENTRIES, 384), bf16)],
        compiler_params=pltpu.CompilerParams(vmem_limit_bytes=VMEM),
        name="pack",
    )(member, peer, positions, spacing, crossings)


def sine_of_turns(y):
    z = y * y
    value = SIN_TERMS[-1]
    for term in SIN_TERMS[-2::-1]:
        value = value * z + term
    return value * y


def put_row(wave_ref, row, values):
    wave_ref[row * PITCH : row * PITCH + ROWS, :] = values


def encode_into(enc_ref, kept_ref, wave_ref, recv_ref, slot):
    pair = slot // 2
    near_side = (iota((ROWS, 128), 1) < SAMPLES) == (slot == 2 * pair)
    points = jnp.concatenate(
        [
            jnp.where(
                near_side,
                recv_ref[:ROWS, 0, wire_row(3 * pair + c)],
                recv_ref[ROWS:, 0, wire_row(3 * pair + c)],
            )
            for c in range(3)
        ],
        axis=0,
    )
    for k in range(FREQS):
        if k % ANCHOR == 0:
            turns = points * (0.5 * 2.0**k)
            turns = turns - jnp.round(turns)
            size = jnp.abs(turns)
            cosine = sine_of_turns(0.25 - size)
            sine = sine_of_turns(jnp.minimum(size, 0.5 - size))
            sine = jnp.where(turns < 0.0, -sine, sine)
        else:
            square = sine * sine
            sine = sine * cosine
            sine = sine + sine
            cosine = 1.0 - (square + square)
        for c in range(3):
            put_row(wave_ref, 6 * k + c, sine[c * ROWS : (c + 1) * ROWS])
            put_row(wave_ref, 6 * k + 3 + c, cosine[c * ROWS : (c + 1) * ROWS])
    for r in range(ROWS):
        lanes = slice(128 * r, 128 * r + 128)
        waves = wave_ref[pl.ds(r, 64, stride=PITCH), :].astype(bf16)
        enc_ref[:, lanes] = waves
        kept_ref[slot, :, lanes] = waves


def in_turns(used_ref, count, prepare, work, buffers):
    here, other = buffers
    prepare(here, used_ref[0])

    def turn(number, carry):
        place = 2 * number
        prepare(other, used_ref[place + 1])
        work(here, used_ref[place])

        @pl.when(place + 1 < count)
        def _():
            prepare(here, used_ref[place + 2])
            work(other, used_ref[place + 1])

        return carry

    lax.fori_loop(0, (count + 1) // 2, turn, 0)


def spread(near, far, slot, lane_index):
    near_side = (iota((ROWS, 128), 1) < SAMPLES) == (slot % 2 == 0)
    return jnp.where(
        near_side, near[:, lane_index : lane_index + 1], far[:, lane_index : lane_index + 1]
    )


def same_half():
    i = iota((128, 128), 0)
    j = iota((128, 128), 1)
    return i, j, (i < SAMPLES) == (j < SAMPLES)


def as_matrix(mask):
    return jnp.where(mask, 1.0, 0.0)


def forward_kernel(*refs):
    recv_ref = refs[0]
    weight_refs = refs[1 : 1 + GROUP]
    small_ref, saved_ref, step_ref, kept_ref, used_ref = refs[1 + GROUP : 6 + GROUP]
    w_ref, head_ref, enc_ref, next_ref, wave_ref, out_ref = refs[6 + GROUP :]

    for i in range(GROUP):
        packed = weight_refs[i][...]
        w_ref[i] = (0.5 * packed).T.astype(bf16)
        head_ref[i] = packed[48:64].astype(bf16)

    near = recv_ref[:ROWS, 0, wire_row(STEP_ROW)]
    far = recv_ref[ROWS:, 0, wire_row(STEP_ROW)]
    most = jnp.max(jnp.maximum(near, far), axis=0, keepdims=True)
    count = jnp.int32(0)
    for place in range(LIST):
        used_ref[place] = 0
    for slot in range(SLOTS):
        used_ref[count] = slot
        count += (most[0, slot] > 0.0).astype(jnp.int32)
    used_ref[LIST] = count
    lane = iota((ROWS, 128), 1)
    turned = pltpu.roll(far, SAMPLES, 1)
    chosen = [
        jnp.where(lane == slot, near, jnp.where(lane == slot + SAMPLES, turned, 0.0))
        for slot in range(SLOTS)
    ]
    i, j, same = same_half()
    steps = add_lanes(jnp.concatenate(chosen, axis=0), same == (i % 2 == 0))
    step_ref[...] = steps.reshape(SLOTS, ROWS, 128)
    out_ref[...] = jnp.zeros((4, SLOTS, ROWS, 128), f32)

    def network(enc_ref, slot):
        first = w_ref[slot // CAP]
        head = head_ref[slot // CAP]
        for n in range(TILE // FORWARD_CHUNK):
            encoded = enc_ref[:, n * FORWARD_CHUNK : (n + 1) * FORWARD_CHUNK]
            half = jnp.dot(first, encoded, preferred_element_type=f32)
            hidden = (half + half * jnp.tanh(half)).astype(bf16)
            output = jnp.dot(head, hidden, preferred_element_type=f32)
            for r in range(FORWARD_CHUNK // 128):
                row = n * (FORWARD_CHUNK // 128) + r
                for v in range(4):
                    out_ref[v, slot, row : row + 1, :] = output[
                        12 + v : 13 + v, 128 * r : 128 * r + 128
                    ]

    wave_ref[...] = jnp.zeros(wave_ref.shape, f32)

    def prepare(ref, slot):
        encode_into(ref, kept_ref, wave_ref, recv_ref, slot)

    in_turns(used_ref, count, prepare, network, (enc_ref, next_ref))

    rows = SLOTS * ROWS
    outputs = [out_ref[v].reshape(rows, 128) for v in range(4)]
    raw = outputs[0]
    density = jnp.maximum(raw, 0.0) + jnp.log1p(jnp.exp(-jnp.abs(raw)))
    optical = density * steps
    inclusive = add_lanes(optical, same & (i <= j))
    leaving = jnp.exp(-inclusive)
    weight = jnp.exp(optical - inclusive) - leaving
    saved_ref[3] = jax.nn.sigmoid(raw).reshape(SLOTS, ROWS, 128)
    saved_ref[4] = weight.reshape(SLOTS, ROWS, 128)
    saved_ref[5] = leaving.reshape(SLOTS, ROWS, 128)
    i = iota((128, 256), 0)
    first_half = iota((128, 256), 1) < 128
    results = []
    for v in range(3):
        colour = jax.nn.sigmoid(outputs[1 + v])
        saved_ref[v] = colour.reshape(SLOTS, ROWS, 128)
        results.append(add_lanes(weight * colour, (i < SAMPLES) == first_half))
    results.append(add_lanes(leaving, i == jnp.where(first_half, SAMPLES - 1, 127)))
    for side in range(2):
        gathered = jnp.zeros((ROWS, 128), f32)
        for v in range(4):
            for slot in range(SLOTS):
                half = (side + slot) % 2
                block = results[v][slot * ROWS : (slot + 1) * ROWS, 128 * half : 128 * half + 128]
                gathered = jnp.where(lane == v * SLOTS + slot, block, gathered)
        small_ref[side * ROWS : (side + 1) * ROWS, :] = gathered


def forward(received, weights):
    vmem = pl.BlockSpec(memory_space=pltpu.VMEM)
    smem = pl.BlockSpec(memory_space=pltpu.SMEM)
    return pl.pallas_call(
        forward_kernel,
        out_shape=(
            jax.ShapeDtypeStruct((PEERS, 128), f32),
            jax.ShapeDtypeStruct((6, SLOTS, ROWS, 128), f32),
            jax.ShapeDtypeStruct((SLOTS, ROWS, 128), f32),
            jax.ShapeDtypeStruct((SLOTS, 64, TILE), bf16),
            jax.ShapeDtypeStruct((LIST + 1,), jnp.int32),
        ),
        in_specs=[vmem] * (1 + GROUP),
        out_specs=(vmem, vmem, vmem, vmem, smem),
        scratch_shapes=[
            pltpu.VMEM((GROUP, HIDDEN, 64), bf16),
            pltpu.VMEM((GROUP, 16, HIDDEN), bf16),
            pltpu.VMEM((64, TILE), bf16),
            pltpu.VMEM((64, TILE), bf16),
            pltpu.VMEM((64 * PITCH, 128), f32),
            pltpu.VMEM((4, SLOTS, ROWS, 128), f32),
        ],
        compiler_params=pltpu.CompilerParams(vmem_limit_bytes=SOME_VMEM),
        cost_estimate=matrix_cost(SLOTS * 2),
        name="forward",
    )(received, *weights)


def ray_kernel(small_ref, index_ref, dest_ref, target_ref, grads_ref, rendered_ref):
    lane = iota((ENTRIES, 128), 1)
    value = lane // SLOTS
    slot = (lane - value * SLOTS).astype(f32)
    dest_col = index_ref[:, 0:1]
    slot_col = index_ref[:, 64:65]
    to_entry = jnp.where(lane.astype(f32) == dest_col, 1.0, 0.0).astype(bf16)
    small = jnp.concatenate([small_ref[...], jnp.zeros((128 - PEERS, 128), f32)], axis=0)
    mine = (slot == slot_col) & (value < 4)
    found = jnp.where(mine, pick(to_entry, small), 0.0)
    i = iota((128, 128), 0)
    j = iota((128, 128), 1)
    segments = add_lanes(found, (i // SLOTS == j) & (j < 4))

    lane = iota((RAYS, 128), 1)
    parts = [segments[s * RAYS : (s + 1) * RAYS] for s in range(SEGS)]
    trans = [jnp.broadcast_to(part[:, 3:4], (RAYS, 128)) for part in parts]
    prefix = [jnp.ones((RAYS, 128), f32)]
    for s in range(SEGS - 1):
        prefix.append(prefix[s] * trans[s])
    rendered = prefix[0] * parts[0]
    for s in range(1, SEGS):
        rendered += prefix[s] * parts[s]
    target = jnp.concatenate([target_ref[...], jnp.zeros((3, 128 - RAYS), f32)], axis=1)
    target = jnp.concatenate([target, jnp.zeros((125, 128), f32)], axis=0).T[:RAYS]
    residual = jnp.where(lane < 3, rendered - target, 0.0)
    behind = jnp.zeros((RAYS, 128), f32)
    grads = [None] * SEGS
    for s in range(SEGS - 1, -1, -1):
        through = prefix[s] * jnp.sum(behind * residual, axis=1, keepdims=True)
        grads[s] = jnp.where(lane == 3, through, prefix[s] * residual)
        behind = parts[s] + trans[s] * behind
    spread_back = add_lanes(jnp.concatenate(grads, axis=0), (j // SLOTS == i) & (i < 4))
    to_dest = jnp.where(iota((PEERS, ENTRIES), 0).astype(f32) == dest_ref[0:1, :], 1.0, 0.0)
    grads_ref[...] = pick(to_dest.astype(bf16), jnp.where(mine, spread_back, 0.0))
    eye = as_matrix(iota((8, 128), 0) == iota((8, 128), 1))
    rendered_ref[...] = nt_dot(eye, rendered, lax.Precision.HIGHEST)[0:3]


def ray_level(small, index, dest, target):
    return pl.pallas_call(
        ray_kernel,
        out_shape=(
            jax.ShapeDtypeStruct((PEERS, 128), f32),
            jax.ShapeDtypeStruct((3, RAYS), f32),
        ),
        compiler_params=pltpu.CompilerParams(vmem_limit_bytes=SOME_VMEM),
        name="rays",
    )(small, index, dest, target)


def upstream_into(up_ref, grads_ref, saved_ref, step_ref):
    near = grads_ref[:ROWS]
    far = grads_ref[ROWS:]
    for v in range(4):
        for slot in range(SLOTS):
            up_ref[v, slot] = spread(near, far, slot, v * SLOTS + slot)

    rows = SLOTS * ROWS

    def flat(x):
        return x.reshape(rows, 128)

    i, j, same = same_half()
    weight = flat(saved_ref[4])
    leaving = flat(saved_ref[5])
    shading = flat(saved_ref[0]) * flat(up_ref[0])
    shading += flat(saved_ref[1]) * flat(up_ref[1])
    shading += flat(saved_ref[2]) * flat(up_ref[2])
    after = add_lanes(weight * shading, same & (i > j))
    last = add_lanes(leaving, same & ((i == SAMPLES - 1) | (i == 127)))
    grad_depth = shading * leaving - after - flat(up_ref[3]) * last
    upstream = [grad_depth * flat(step_ref[...]) * flat(saved_ref[3])]
    for v in range(3):
        colour = flat(saved_ref[v])
        upstream.append(weight * flat(up_ref[v]) * colour * (1.0 - colour))
    for v in range(4):
        up_ref[v] = upstream[v].reshape(SLOTS, ROWS, 128)


def backward_kernel(*refs):
    member_ref, grads_ref, saved_ref, step_ref, kept_ref, used_ref = refs[:6]
    weight_refs = refs[6 : 6 + GROUP]
    total_ref, up_ref, both_ref, sum_ref, input_ref, next_ref, wave_ref, right_ref = refs[
        6 + GROUP :
    ]
    both_ref[...] = jnp.zeros(both_ref.shape, bf16)
    for i in range(GROUP):
        packed = (0.5 * weight_refs[i][...]).astype(bf16)
        both_ref[i, :64, :HIDDEN] = packed
        both_ref[i, 64:, HIDDEN:] = packed[48:]
    sum_ref[...] = jnp.zeros(sum_ref.shape, f32)
    upstream_into(up_ref, grads_ref, saved_ref, step_ref)
    wave_ref[...] = jnp.zeros(wave_ref.shape, f32)

    def prepare(ref, slot):
        for v in range(4):
            put_row(wave_ref, 12 + v, up_ref[v, slot])
        for r in range(ROWS):
            ref[:, 128 * r : 128 * r + 128] = wave_ref[pl.ds(r, 16, stride=PITCH), :].astype(bf16)

    def work(ref, slot):
        brick = slot // CAP
        both = both_ref[brick]
        for n in range(TILE // BACKWARD_CHUNK):
            chunk = slice(n * BACKWARD_CHUNK, (n + 1) * BACKWARD_CHUNK)
            given = jnp.concatenate([kept_ref[slot, :, chunk], ref[:, chunk]], axis=0)
            product = tn_dot(given, both)
            half = product[:, :HIDDEN]
            bend = jnp.tanh(half)
            bent = half * bend
            slope = (1.0 + bend) * ((1.0 + half) - bent)
            right_ref[chunk, HIDDEN:] = (half + bent).astype(bf16)
            right_ref[chunk, :HIDDEN] = (product[:, HIDDEN:] * slope).astype(bf16)
        given = jnp.concatenate([kept_ref[slot], ref[...]], axis=0)
        sum_ref[brick] += jnp.dot(given, right_ref[...], preferred_element_type=f32)

    in_turns(used_ref, used_ref[LIST], prepare, work, (input_ref, next_ref))
    for i in range(GROUP):
        member = lax.rem(member_ref[0] + i, GROUP)
        total_ref[member, :48] = sum_ref[i, :48, :HIDDEN]
        total_ref[member, 48:] = sum_ref[i, 48:64, :HIDDEN] + sum_ref[i, 64:, HIDDEN:]


def backward(member, grads, saved, steps, kept, used, weights):
    vmem = pl.BlockSpec(memory_space=pltpu.VMEM)
    smem = pl.BlockSpec(memory_space=pltpu.SMEM)
    return pl.pallas_call(
        backward_kernel,
        out_shape=jax.ShapeDtypeStruct((GROUP, 64, HIDDEN), f32),
        in_specs=[smem, vmem, vmem, vmem, vmem, smem] + [vmem] * GROUP,
        out_specs=vmem,
        scratch_shapes=[
            pltpu.VMEM((4, SLOTS, ROWS, 128), f32),
            pltpu.VMEM((GROUP, 80, 2 * HIDDEN), bf16),
            pltpu.VMEM((GROUP, 80, 2 * HIDDEN), f32),
            pltpu.VMEM((16, TILE), bf16),
            pltpu.VMEM((16, TILE), bf16),
            pltpu.VMEM((16 * PITCH, 128), f32),
            pltpu.VMEM((TILE, 2 * HIDDEN), bf16),
        ],
        compiler_params=pltpu.CompilerParams(vmem_limit_bytes=SOME_VMEM),
        cost_estimate=matrix_cost(SLOTS * 4),
        name="backward",
    )(member, grads, saved, steps, kept, used, *weights)


def sum_kernel(*refs):
    parts_ref, total_ref, square_ref = refs
    total = parts_ref[0]
    for i in range(1, GROUP):
        total += parts_ref[i]
    total_ref[...] = total
    square = jnp.sum(jnp.sum(total * total, axis=1, keepdims=True), axis=0, keepdims=True)
    square_ref[...] = jnp.broadcast_to(square, square_ref.shape)


def add_up(partials, bricks):
    return pl.pallas_call(
        sum_kernel,
        out_shape=(
            jax.ShapeDtypeStruct((64, HIDDEN), f32),
            jax.ShapeDtypeStruct((bricks, 128), f32),
        ),
        compiler_params=pltpu.CompilerParams(vmem_limit_bytes=SOME_VMEM),
        name="add_up",
    )(partials)


def normalize(total, squares, count):
    def body(total_ref, squares_ref, first_ref, head_ref):
        overall = jnp.sum(squares_ref[:, 0:1], axis=0, keepdims=True)
        scaled = total_ref[...] * lax.rsqrt(overall / count + NORM_EPS)
        first_ref[:, 0, :] = scaled[: 6 * FREQS]
        head_ref[0] = scaled[6 * FREQS :]

    first, head = pl.pallas_call(
        body,
        out_shape=(
            jax.ShapeDtypeStruct((6 * FREQS, 1, HIDDEN), f32),
            jax.ShapeDtypeStruct((1, 4, HIDDEN), f32),
        ),
        compiler_params=pltpu.CompilerParams(vmem_limit_bytes=SOME_VMEM),
        name="normalize",
    )(total, squares)
    return first.transpose(1, 2, 0), head


def from_ahead(x, distance):
    return lax.ppermute(x, GROUP_AXIS, [(i, (i - distance) % GROUP) for i in range(GROUP)])


def exchange(x, axes):
    return lax.all_to_all(x, axes, split_axis=0, concat_axis=0, tiled=True)


def on_device(positions, spacing, crossings, target, first_weight, head_weight):
    own = jnp.concatenate(
        [first_weight[0].astype(f32).T, head_weight[0].astype(f32)], axis=0
    )
    weights = [own] + [from_ahead(own, distance) for distance in range(1, GROUP)]
    bricks = GROUP * PEERS
    member = lax.axis_index(GROUP_AXIS).astype(jnp.int32).reshape(1)
    peer = lax.axis_index(PEER_AXES).astype(jnp.int32).reshape(1)
    send, index, dest = pack(member, peer, positions, spacing.T, crossings.T)
    received = exchange(send, PEER_AXES)
    small, saved, steps, kept, used = forward(received, weights)
    grads, rendered = ray_level(exchange(small, PEER_AXES), index, dest, target)
    grads = exchange(grads, PEER_AXES)
    partials = backward(member, grads, saved, steps, kept, used, weights)
    total, square = add_up(exchange(partials, GROUP_AXIS), bricks)
    squares = exchange(square, ALL)
    first_update, head_update = normalize(total, squares, bricks * (64 * HIDDEN))
    return (rendered, first_update, head_update)


def solution(mesh):
    in_specs = (
        P(None, ALL, None),
        P(ALL, None),
        P(ALL, None),
        P(None, ALL),
        P(ALL, None, None),
        P(ALL, None, None),
    )
    out_specs = (P(None, ALL), P(ALL, None, None), P(ALL, None, None))
    return jax.shard_map(
        on_device, mesh=mesh, in_specs=in_specs, out_specs=out_specs, check_vma=False
    )
```

time: 160 us -> 131 us (0.82); the launches traced: 161 us -> 130 us
  blocking collectives: 38.3 us -> 65.7 us
  starting transfers between devices: 45.1 us -> 21.7 us
  waiting for transfers between devices: 23.1 us -> 7.14 us
  Pallas kernels: 49.9 us -> 34 us
  local copies, waits for them, and re-layouts: 2.81 us -> 0.02 us
    all_to_all x2 -> x4, blocking collectives: 38.3 us -> 65.7 us  [exchange(): return lax.all_to_all(x, axes, split_axis=0, concat_axis=0, tiled=True)]
    ppermute x14 -> x7, starting transfers between devices: 24.4 us -> 9.85 us  [from_ahead(): lax.ppermute(x, GROUP_AXIS, [(i, (i - distance) % GROUP) for i in range(G...]
    all_to_all x2 -> x1, waiting for transfers between devices: 13.4 us -> 3.92 us  [exchange(): return lax.all_to_all(x, axes, split_axis=0, concat_axis=0, tiled=True)]
    all_to_all x2 -> x1, starting transfers between devices: 20.7 us -> 11.9 us  [exchange(): return lax.all_to_all(x, axes, split_axis=0, concat_axis=0, tiled=True)]
    pallas_call x3 -> x2, Pallas kernels: 28 us -> 20.3 us  [the longest x1 16.6 us: backward(): pl.pallas_call(backward_kernel, out_shape=jax.ShapeDtypeStruct((GROUP, 64...]
    ppermute x14 -> x7, waiting for transfers between devices: 9.7 us -> 3.22 us  [from_ahead(): lax.ppermute(x, GROUP_AXIS, [(i, (i - distance) % GROUP) for i in range(G...]
    pallas_call x1, Pallas kernels: 15.1 us -> 10.9 us  [forward(): pl.pallas_call(forward_kernel, out_shape=(jax.ShapeDtypeStruct((PEERS, 12...]
    unnamed x49 -> x6, local copies, waits for them, and re-layouts: 2.2 us -> 0.02 us
  transfers between devices with their start and end apart: 16 -> 8, of which waited for: 9 -> 4; matrix products, arithmetic and copies ran while one was open for 0% -> 1% of each run, Pallas kernels for 0% -> 0%
where the time goes in v2:
time: 131 us; the launch traced here: 130 us
  blocking collectives  65.7 us (50%)
  Pallas kernels  34 us (26%)
  starting transfers between devices  21.7 us (17%)
  waiting for transfers between devices  7.14 us (5%)
    all_to_all x4, blocking collectives, exchange(): return lax.all_to_all(x, axes, split_axis=0, concat_axis=0, tiled=True)  65.7 us
    pallas_call x1, Pallas kernels, backward(): pl.pallas_call(backward_kernel, out_shape=jax.ShapeDtypeStruct((GROUP, 64...  16.6 us
    all_to_all x1, starting transfers between devices, exchange(): return lax.all_to_all(x, axes, split_axis=0, concat_axis=0, tiled=True)  11.9 us
    pallas_call x1, Pallas kernels, forward(): pl.pallas_call(forward_kernel, out_shape=(jax.ShapeDtypeStruct((PEERS, 12...  10.9 us
    ppermute x7, starting transfers between devices, from_ahead(): lax.ppermute(x, GROUP_AXIS, [(i, (i - distance) % GROUP) for i in range(G...  9.85 us
    all_to_all x1, waiting for transfers between devices, exchange(): return lax.all_to_all(x, axes, split_axis=0, concat_axis=0, tiled=True)  3.92 us
    pallas_call x1, Pallas kernels, pack(): pl.pallas_call(pack_kernel, out_shape=(jax.ShapeDtypeStruct((PEERS, 1, 12...  3.68 us
    ppermute x7, waiting for transfers between devices, from_ahead(): lax.ppermute(x, GROUP_AXIS, [(i, (i - distance) % GROUP) for i in range(G...  3.22 us
  transfers between devices with their start and end apart: 8, of which 4 were waited for; matrix products, arithmetic and copies ran while one was open for 1% of the time, Pallas kernels for 0%

profile of v2, /device:TPU:1, one launch (start us, length us, event | category | flops | bytes accessed | tf_op | source)
XLA Modules:
  0.0 130.0 jit_solution(6910582230598994884)
XLA Ops:
  0.6 3.7 %pack.1 = (f32[32,1,4736]{2,1,0:T(1,128)}, f32[384,128]{1,0:T(8,128)}, f32[8,384]{1,0:T(8,128)}) custom-call(s32[1]{0:T(128)} %bitcast.member_ref.refs_0_, s32[1]{0:T(128)} %bitcast.1.peer_ref, f32[3,48,512]{2,1,0:T(8,128)} %pos_ref.1, f32[8,48]{1,0:T(8,128)} %bitcast.28, s32[8,48]{1,0:T(8,128)} %bitcast.29), custom_call_target="tpu_custom_call" | custom-call | tf_op jit(solution)/shard_map/pack/pallas_call | solution.py:163
  4.3 11.9 %all-to-all-start = ((f32[32,1,4736]{2,1,0:T(1,128)}), f32[32,1,4736]{2,1,0:T(1,128)S(1)}, u32[]{:S(2)}, u32[]{:S(2)}) async-start(f32[32,1,4736]{2,1,0:T(1,128)} %get-tuple-element.17), calls=%async_computation | async-start | bytes 1212416 | tf_op jit(solution)/shard_map/all_to_all | solution.py:567
  16.2 0.8 maximum_convert_fusion.refs_1_.refs_6_
  17.0 0.0 copy-start.1
  17.0 0.0 copy-start.2
  17.0 2.1 %collective-permute-start.6 = (f32[64,256]{1,0:T(8,128)S(1)}, f32[64,256]{1,0:T(8,128)S(1)}, u32[]{:S(2)}, u32[]{:S(2)}) collective-permute-start(f32[64,256]{1,0:T(8,128)S(1)} %maximum_convert_fusion.refs_1_.refs_6_), channel_id=1, source_target_pairs={{0,1},{1,2},{2,3},{3,4},{4,5},{5,6},{6,7},{7,0},{8,9},{9,10},{10,1... | collective-permute-start | bytes 196616 | tf_op jit(solution)/shard_map/ppermute | solution.py:563
  19.2 1.3 collective-permute-start.5
  20.4 1.7 %collective-permute-start.4 = (f32[64,256]{1,0:T(8,128)S(1)}, f32[64,256]{1,0:T(8,128)S(1)}, u32[]{:S(2)}, u32[]{:S(2)}) collective-permute-start(f32[64,256]{1,0:T(8,128)S(1)} %maximum_convert_fusion.refs_1_.refs_6_), channel_id=1, source_target_pairs={{0,3},{1,4},{2,5},{3,6},{4,7},{5,0},{6,1},{7,2},{8,11},{9,12},{10,... | collective-permute-start | bytes 196616 | tf_op jit(solution)/shard_map/ppermute | solution.py:563
  22.1 0.3 collective-permute-start.3
  22.5 1.9 %collective-permute-start.2 = (f32[64,256]{1,0:T(8,128)S(1)}, f32[64,256]{1,0:T(8,128)S(1)}, u32[]{:S(2)}, u32[]{:S(2)}) collective-permute-start(f32[64,256]{1,0:T(8,128)S(1)} %maximum_convert_fusion.refs_1_.refs_6_), channel_id=1, source_target_pairs={{0,5},{1,6},{2,7},{3,0},{4,1},{5,2},{6,3},{7,4},{8,13},{9,14},{10,... | collective-permute-start | bytes 196616 | tf_op jit(solution)/shard_map/ppermute | solution.py:563
  24.4 0.0 collective-permute-done.6.refs_8_.refs_13_
  24.4 0.8 collective-permute-start.1
  25.3 0.0 collective-permute-done.5.refs_7_.refs_12_
  25.3 1.6 %collective-permute-start = (f32[64,256]{1,0:T(8,128)S(1)}, f32[64,256]{1,0:T(8,128)S(1)}, u32[]{:S(2)}, u32[]{:S(2)}) collective-permute-start(f32[64,256]{1,0:T(8,128)S(1)} %maximum_convert_fusion.refs_1_.refs_6_), channel_id=1, source_target_pairs={{0,7},{1,0},{2,1},{3,2},{4,3},{5,4},{6,5},{7,6},{8,15},{9,8},{10,9... | collective-permute-start | bytes 196616 | tf_op jit(solution)/shard_map/ppermute | solution.py:563
  26.9 0.0 collective-permute-done.4.refs_6_.refs_11_
  26.9 1.0 collective-permute-done.3.refs_5_.refs_10_
  27.9 0.8 collective-permute-done.2.refs_4_.refs_9_
  28.6 0.0 collective-permute-done.1.refs_3_.refs_8_
  28.6 1.5 %collective-permute-done.refs_2_.refs_7_ = f32[64,256]{1,0:T(8,128)S(1)} collective-permute-done((f32[64,256]{1,0:T(8,128)S(1)}, f32[64,256]{1,0:T(8,128)S(1)}, u32[]{:S(2)}, u32[]{:S(2)}) %collective-permute-start) | collective-permute-done | bytes 65568 | tf_op jit(solution)/shard_map/ppermute | solution.py:563
  30.1 3.9 %all-to-all-done.refs_0_ = f32[32,1,4736]{2,1,0:T(1,128)S(1)} async-done(((f32[32,1,4736]{2,1,0:T(1,128)}), f32[32,1,4736]{2,1,0:T(1,128)S(1)}, u32[]{:S(2)}, u32[]{:S(2)}) %all-to-all-start) | async-done | bytes 606240 | tf_op jit(solution)/shard_map/all_to_all | solution.py:567
  34.0 10.9 %forward.1 = (f32[32,128]{1,0:T(8,128)S(1)}, f32[6,24,16,128]{3,2,1,0:T(8,128)S(1)}, f32[24,16,128]{2,1,0:T(8,128)S(1)}, bf16[24,64,2048]{2,1,0:T(8,128)(2,1)S(1)}, s32[27]{0:T(128)S(1)}) custom-call(f32[32,1,4736]{2,1,0:T(1,128)S(1)} %all-to-all-done.refs_0_, f32[64,256]{1,0:T(8,128)S(1)} %maximum_convert_fusion.refs_1_.refs_6_, ...), custom_call_target="tpu_custom_call" | custom-call | flops 12884901888 | bytes 4194304 | tf_op jit(solution)/shard_map/forward/pallas_call | solution.py:349
  44.9 16.1 %all_to_all.43 = f32[32,1,128]{2,1,0:T(1,128)S(1)} all-to-all(f32[32,1,128]{2,1,0:T(1,128)S(1)} %bitcast.25), channel_id=1, replica_groups=mesh['gx'=8,'gy'=4,'gz'=8] {'gx','gy'}, dimensions={0} | all-to-all | bytes 32768 | tf_op jit(solution)/shard_map/all_to_all | solution.py:567
  61.0 0.0 copy-done
  61.0 0.0 copy-done.1
  61.0 0.0 copy-done.2
  61.0 1.9 %rays.1 = (f32[32,128]{1,0:T(8,128)S(1)}, f32[3,48]{1,0:T(4,128)}) custom-call(f32[32,128]{1,0:T(8,128)S(1)} %bitcast.23, f32[384,128]{1,0:T(8,128)S(1)} %copy-done, f32[8,384]{1,0:T(8,128)S(1)} %copy-done.1, f32[3,48]{1,0:T(4,128)S(1)} %copy-done.2), custom_call_target="tpu_custom_call" | custom-call | tf_op jit(solution)/shard_map/rays/pallas_call | solution.py:414
  62.9 11.5 %all_to_all.44 = f32[32,1,128]{2,1,0:T(1,128)S(1)} all-to-all(f32[32,1,128]{2,1,0:T(1,128)S(1)} %bitcast.26), channel_id=1, replica_groups=mesh['gx'=8,'gy'=4,'gz'=8] {'gx','gy'}, dimensions={0} | all-to-all | bytes 32768 | tf_op jit(solution)/shard_map/all_to_all | solution.py:567
  74.4 16.6 %backward.1 = f32[8,64,256]{2,1,0:T(8,128)S(1)} custom-call(s32[1]{0:T(128)} %bitcast.member_ref.refs_0_, f32[32,128]{1,0:T(8,128)S(1)} %bitcast.24, f32[6,24,16,128]{3,2,1,0:T(8,128)S(1)} %get-tuple-element.23.refs_2_, f32[24,16,128]{2,1,0:T(8,128)S(1)} %get-tuple-element.24.refs_3_, bf16[24,64,2048]{2,1,0:T(8,128)(2,1)S(1)} %get-tuple-element.25.refs_4_, ...), custom_call_target="tpu_custom_call" | custom-call | flops 25769803776 | bytes 4194304 | tf_op jit(solution)/shard_map/backward/pallas_call | solution.py:501
  91.0 18.2 %all_to_all.45.refs_0_ = f32[8,64,256]{2,1,0:T(8,128)S(1)} all-to-all(f32[8,64,256]{2,1,0:T(8,128)S(1)} %backward.1), channel_id=1, replica_groups=mesh['gx'=8,'gy'=4,'gz'=8] {'gz'}, dimensions={0} | all-to-all | bytes 1048576 | tf_op jit(solution)/shard_map/all_to_all | solution.py:567
  109.3 0.1 add_up.1
  109.4 19.9 %all_to_all.46 = f32[256,1,128]{2,1,0:T(1,128)S(1)} all-to-all(f32[256,1,128]{2,1,0:T(1,128)S(1)} %bitcast.22), channel_id=1, replica_groups=mesh['gx'=8,'gy'=4,'gz'=8] {'gx','gy','gz'}, dimensions={0} | all-to-all | bytes 262144 | tf_op jit(solution)/shard_map/all_to_all | solution.py:567
  129.2 0.8 normalize.1
  (1 shorter events, 0.0 us)
Async XLA Ops:
  4.3 29.7 %all-to-all-start = ((f32[32,1,4736]{2,1,0:T(1,128)}), f32[32,1,4736]{2,1,0:T(1,128)S(1)}, u32[]{:S(2)}, u32[]{:S(2)}) async-start(f32[32,1,4736]{2,1,0:T(1,128)} %get-tuple-element.17), calls=%async_computation | async-start | bytes 1212416 | tf_op jit(solution)/shard_map/all_to_all | solution.py:567
  17.0 44.0 %copy-start = (f32[384,128]{1,0:T(8,128)S(1)}, f32[384,128]{1,0:T(8,128)}, u32[]{:S(2)}) copy-start(f32[384,128]{1,0:T(8,128)} %get-tuple-element.19.index_ref) | copy-start | bytes 589828
  17.0 44.0 %copy-start.1 = (f32[8,384]{1,0:T(8,128)S(1)}, f32[8,384]{1,0:T(8,128)}, u32[]{:S(2)}) copy-start(f32[8,384]{1,0:T(8,128)} %get-tuple-element.20.dest_ref) | copy-start | bytes 36868
  17.0 44.0 %copy-start.2 = (f32[3,48]{1,0:T(4,128)S(1)}, f32[3,48]{1,0:T(4,128)}, u32[]{:S(2)}) copy-start(f32[3,48]{1,0:T(4,128)} %target_ref.1) | copy-start | bytes 1732
  17.0 7.4 %collective-permute-start.6 = (f32[64,256]{1,0:T(8,128)S(1)}, f32[64,256]{1,0:T(8,128)S(1)}, u32[]{:S(2)}, u32[]{:S(2)}) collective-permute-start(f32[64,256]{1,0:T(8,128)S(1)} %maximum_convert_fusion.refs_1_.refs_6_), channel_id=1, source_target_pairs={{0,1},{1,2},{2,3},{3,4},{4,5},{5,6},{6,7},{7,0},{8,9},{9,10},{10,1... | collective-permute-start | bytes 196616 | tf_op jit(solution)/shard_map/ppermute | solution.py:563
  19.2 6.1 %collective-permute-start.5 = (f32[64,256]{1,0:T(8,128)S(1)}, f32[64,256]{1,0:T(8,128)S(1)}, u32[]{:S(2)}, u32[]{:S(2)}) collective-permute-start(f32[64,256]{1,0:T(8,128)S(1)} %maximum_convert_fusion.refs_1_.refs_6_), channel_id=1, source_target_pairs={{0,2},{1,3},{2,4},{3,5},{4,6},{5,7},{6,0},{7,1},{8,10},{9,11},{10,... | collective-permute-start | bytes 196616 | tf_op jit(solution)/shard_map/ppermute | solution.py:563
  20.4 6.4 %collective-permute-start.4 = (f32[64,256]{1,0:T(8,128)S(1)}, f32[64,256]{1,0:T(8,128)S(1)}, u32[]{:S(2)}, u32[]{:S(2)}) collective-permute-start(f32[64,256]{1,0:T(8,128)S(1)} %maximum_convert_fusion.refs_1_.refs_6_), channel_id=1, source_target_pairs={{0,3},{1,4},{2,5},{3,6},{4,7},{5,0},{6,1},{7,2},{8,11},{9,12},{10,... | collective-permute-start | bytes 196616 | tf_op jit(solution)/shard_map/ppermute | solution.py:563
  22.1 5.7 %collective-permute-start.3 = (f32[64,256]{1,0:T(8,128)S(1)}, f32[64,256]{1,0:T(8,128)S(1)}, u32[]{:S(2)}, u32[]{:S(2)}) collective-permute-start(f32[64,256]{1,0:T(8,128)S(1)} %maximum_convert_fusion.refs_1_.refs_6_), channel_id=1, source_target_pairs={{0,4},{1,5},{2,6},{3,7},{4,0},{5,1},{6,2},{7,3},{8,12},{9,13},{10,... | collective-permute-start | bytes 196616 | tf_op jit(solution)/shard_map/ppermute | solution.py:563
  22.5 6.1 %collective-permute-start.2 = (f32[64,256]{1,0:T(8,128)S(1)}, f32[64,256]{1,0:T(8,128)S(1)}, u32[]{:S(2)}, u32[]{:S(2)}) collective-permute-start(f32[64,256]{1,0:T(8,128)S(1)} %maximum_convert_fusion.refs_1_.refs_6_), channel_id=1, source_target_pairs={{0,5},{1,6},{2,7},{3,0},{4,1},{5,2},{6,3},{7,4},{8,13},{9,14},{10,... | collective-permute-start | bytes 196616 | tf_op jit(solution)/shard_map/ppermute | solution.py:563
  24.4 4.2 %collective-permute-start.1 = (f32[64,256]{1,0:T(8,128)S(1)}, f32[64,256]{1,0:T(8,128)S(1)}, u32[]{:S(2)}, u32[]{:S(2)}) collective-permute-start(f32[64,256]{1,0:T(8,128)S(1)} %maximum_convert_fusion.refs_1_.refs_6_), channel_id=1, source_target_pairs={{0,6},{1,7},{2,0},{3,1},{4,2},{5,3},{6,4},{7,5},{8,14},{9,15},{10,... | collective-permute-start | bytes 196616 | tf_op jit(solution)/shard_map/ppermute | solution.py:563
  25.3 4.8 %collective-permute-start = (f32[64,256]{1,0:T(8,128)S(1)}, f32[64,256]{1,0:T(8,128)S(1)}, u32[]{:S(2)}, u32[]{:S(2)}) collective-permute-start(f32[64,256]{1,0:T(8,128)S(1)} %maximum_convert_fusion.refs_1_.refs_6_), channel_id=1, source_target_pairs={{0,7},{1,0},{2,1},{3,2},{4,3},{5,4},{6,5},{7,6},{8,15},{9,8},{10,9... | collective-permute-start | bytes 196616 | tf_op jit(solution)/shard_map/ppermute | solution.py:563

commit v3 on v2

--- a/solution.py
+++ b/solution.py
@@ -454,15 +454,15 @@
 def backward_kernel(*refs):
     member_ref, grads_ref, saved_ref, step_ref, kept_ref, used_ref = refs[:6]
     weight_refs = refs[6 : 6 + GROUP]
-    total_ref, up_ref, both_ref, sum_ref, input_ref, next_ref, wave_ref, right_ref = refs[
-        6 + GROUP :
-    ]
+    total_ref, up_ref, both_ref, first_ref, head_ref, *buffers = refs[6 + GROUP :]
+    input_ref, next_ref, wave_ref, before_ref, hidden_ref = buffers
     both_ref[...] = jnp.zeros(both_ref.shape, bf16)
     for i in range(GROUP):
         packed = (0.5 * weight_refs[i][...]).astype(bf16)
         both_ref[i, :64, :HIDDEN] = packed
         both_ref[i, 64:, HIDDEN:] = packed[48:]
-    sum_ref[...] = jnp.zeros(sum_ref.shape, f32)
+    first_ref[...] = jnp.zeros(first_ref.shape, f32)
+    head_ref[...] = jnp.zeros(head_ref.shape, f32)
     upstream_into(up_ref, grads_ref, saved_ref, step_ref)
     wave_ref[...] = jnp.zeros(wave_ref.shape, f32)
 
@@ -483,16 +483,16 @@
             bend = jnp.tanh(half)
             bent = half * bend
             slope = (1.0 + bend) * ((1.0 + half) - bent)
-            right_ref[chunk, HIDDEN:] = (half + bent).astype(bf16)
-            right_ref[chunk, :HIDDEN] = (product[:, HIDDEN:] * slope).astype(bf16)
-        given = jnp.concatenate([kept_ref[slot], ref[...]], axis=0)
-        sum_ref[brick] += jnp.dot(given, right_ref[...], preferred_element_type=f32)
+            hidden_ref[chunk] = (half + bent).astype(bf16)
+            before_ref[chunk] = (product[:, HIDDEN:] * slope).astype(bf16)
+        first_ref[brick] += jnp.dot(kept_ref[slot], before_ref[...], preferred_element_type=f32)
+        head_ref[brick] += jnp.dot(ref[...], hidden_ref[...], preferred_element_type=f32)
 
     in_turns(used_ref, used_ref[LIST], prepare, work, (input_ref, next_ref))
     for i in range(GROUP):
         member = lax.rem(member_ref[0] + i, GROUP)
-        total_ref[member, :48] = sum_ref[i, :48, :HIDDEN]
-        total_ref[member, 48:] = sum_ref[i, 48:64, :HIDDEN] + sum_ref[i, 64:, HIDDEN:]
+        total_ref[member, :48] = first_ref[i, :48]
+        total_ref[member, 48:] = first_ref[i, 48:] + head_ref[i]
 
 
 def backward(member, grads, saved, steps, kept, used, weights):
@@ -506,11 +506,13 @@
         scratch_shapes=[
             pltpu.VMEM((4, SLOTS, ROWS, 128), f32),
             pltpu.VMEM((GROUP, 80, 2 * HIDDEN), bf16),
-            pltpu.VMEM((GROUP, 80, 2 * HIDDEN), f32),
+            pltpu.VMEM((GROUP, 64, HIDDEN), f32),
+            pltpu.VMEM((GROUP, 16, HIDDEN), f32),
             pltpu.VMEM((16, TILE), bf16),
             pltpu.VMEM((16, TILE), bf16),
             pltpu.VMEM((16 * PITCH, 128), f32),
-            pltpu.VMEM((TILE, 2 * HIDDEN), bf16),
+            pltpu.VMEM((TILE, HIDDEN), bf16),
+            pltpu.VMEM((TILE, HIDDEN), bf16),
         ],
         compiler_params=pltpu.CompilerParams(vmem_limit_bytes=SOME_VMEM),
         cost_estimate=matrix_cost(SLOTS * 4),

time: 131 us -> 130 us (level)
  no operation moved by 1% of the time
where the time goes in v3:
time: 130 us; the launch traced here: 129 us
  blocking collectives  65.9 us (51%)
  Pallas kernels  33.2 us (26%)
  starting transfers between devices  21.7 us (17%)
  waiting for transfers between devices  7.14 us (5%)
    all_to_all x4, blocking collectives, exchange(): return lax.all_to_all(x, axes, split_axis=0, concat_axis=0, tiled=True)  65.9 us
    pallas_call x1, Pallas kernels, backward(): pl.pallas_call(backward_kernel, out_shape=jax.ShapeDtypeStruct((GROUP, 64...  15.8 us
    all_to_all x1, starting transfers between devices, exchange(): return lax.all_to_all(x, axes, split_axis=0, concat_axis=0, tiled=True)  11.9 us
    pallas_call x1, Pallas kernels, forward(): pl.pallas_call(forward_kernel, out_shape=(jax.ShapeDtypeStruct((PEERS, 12...  10.9 us
    ppermute x7, starting transfers between devices, from_ahead(): lax.ppermute(x, GROUP_AXIS, [(i, (i - distance) % GROUP) for i in range(G...  9.85 us
    all_to_all x1, waiting for transfers between devices, exchange(): return lax.all_to_all(x, axes, split_axis=0, concat_axis=0, tiled=True)  3.92 us
    pallas_call x1, Pallas kernels, pack(): pl.pallas_call(pack_kernel, out_shape=(jax.ShapeDtypeStruct((PEERS, 1, 12...  3.68 us
    ppermute x7, waiting for transfers between devices, from_ahead(): lax.ppermute(x, GROUP_AXIS, [(i, (i - distance) % GROUP) for i in range(G...  3.22 us
  transfers between devices with their start and end apart: 8, of which 4 were waited for; matrix products, arithmetic and copies ran while one was open for 1% of the time, Pallas kernels for 0%

profile of v3, /device:TPU:1, one launch (start us, length us, event | category | flops | bytes accessed | tf_op | source)
XLA Modules:
  0.0 129.4 jit_solution(4370325364090890308)
XLA Ops:
  0.6 3.7 %pack.1 = (f32[32,1,4736]{2,1,0:T(1,128)}, f32[384,128]{1,0:T(8,128)}, f32[8,384]{1,0:T(8,128)}) custom-call(s32[1]{0:T(128)} %bitcast.member_ref.refs_0_, s32[1]{0:T(128)} %bitcast.1.peer_ref, f32[3,48,512]{2,1,0:T(8,128)} %pos_ref.1, f32[8,48]{1,0:T(8,128)} %bitcast.28, s32[8,48]{1,0:T(8,128)} %bitcast.29), custom_call_target="tpu_custom_call" | custom-call | tf_op jit(solution)/shard_map/pack/pallas_call | solution.py:163
  4.3 11.9 %all-to-all-start = ((f32[32,1,4736]{2,1,0:T(1,128)}), f32[32,1,4736]{2,1,0:T(1,128)S(1)}, u32[]{:S(2)}, u32[]{:S(2)}) async-start(f32[32,1,4736]{2,1,0:T(1,128)} %get-tuple-element.17), calls=%async_computation | async-start | bytes 1212416 | tf_op jit(solution)/shard_map/all_to_all | solution.py:569
  16.2 0.8 maximum_convert_fusion.refs_1_.refs_6_
  17.0 0.0 copy-start.1
  17.0 0.0 copy-start.2
  17.0 2.1 %collective-permute-start.6 = (f32[64,256]{1,0:T(8,128)S(1)}, f32[64,256]{1,0:T(8,128)S(1)}, u32[]{:S(2)}, u32[]{:S(2)}) collective-permute-start(f32[64,256]{1,0:T(8,128)S(1)} %maximum_convert_fusion.refs_1_.refs_6_), channel_id=1, source_target_pairs={{0,1},{1,2},{2,3},{3,4},{4,5},{5,6},{6,7},{7,0},{8,9},{9,10},{10,1... | collective-permute-start | bytes 196616 | tf_op jit(solution)/shard_map/ppermute | solution.py:565
  19.2 1.3 %collective-permute-start.5 = (f32[64,256]{1,0:T(8,128)S(1)}, f32[64,256]{1,0:T(8,128)S(1)}, u32[]{:S(2)}, u32[]{:S(2)}) collective-permute-start(f32[64,256]{1,0:T(8,128)S(1)} %maximum_convert_fusion.refs_1_.refs_6_), channel_id=1, source_target_pairs={{0,2},{1,3},{2,4},{3,5},{4,6},{5,7},{6,0},{7,1},{8,10},{9,11},{10,... | collective-permute-start | bytes 196616 | tf_op jit(solution)/shard_map/ppermute | solution.py:565
  20.4 1.7 %collective-permute-start.4 = (f32[64,256]{1,0:T(8,128)S(1)}, f32[64,256]{1,0:T(8,128)S(1)}, u32[]{:S(2)}, u32[]{:S(2)}) collective-permute-start(f32[64,256]{1,0:T(8,128)S(1)} %maximum_convert_fusion.refs_1_.refs_6_), channel_id=1, source_target_pairs={{0,3},{1,4},{2,5},{3,6},{4,7},{5,0},{6,1},{7,2},{8,11},{9,12},{10,... | collective-permute-start | bytes 196616 | tf_op jit(solution)/shard_map/ppermute | solution.py:565
  22.1 0.3 collective-permute-start.3
  22.5 1.9 %collective-permute-start.2 = (f32[64,256]{1,0:T(8,128)S(1)}, f32[64,256]{1,0:T(8,128)S(1)}, u32[]{:S(2)}, u32[]{:S(2)}) collective-permute-start(f32[64,256]{1,0:T(8,128)S(1)} %maximum_convert_fusion.refs_1_.refs_6_), channel_id=1, source_target_pairs={{0,5},{1,6},{2,7},{3,0},{4,1},{5,2},{6,3},{7,4},{8,13},{9,14},{10,... | collective-permute-start | bytes 196616 | tf_op jit(solution)/shard_map/ppermute | solution.py:565
  24.4 0.0 collective-permute-done.6.refs_8_.refs_13_
  24.4 0.8 collective-permute-start.1
  25.3 0.0 collective-permute-done.5.refs_7_.refs_12_
  25.3 1.6 %collective-permute-start = (f32[64,256]{1,0:T(8,128)S(1)}, f32[64,256]{1,0:T(8,128)S(1)}, u32[]{:S(2)}, u32[]{:S(2)}) collective-permute-start(f32[64,256]{1,0:T(8,128)S(1)} %maximum_convert_fusion.refs_1_.refs_6_), channel_id=1, source_target_pairs={{0,7},{1,0},{2,1},{3,2},{4,3},{5,4},{6,5},{7,6},{8,15},{9,8},{10,9... | collective-permute-start | bytes 196616 | tf_op jit(solution)/shard_map/ppermute | solution.py:565
  26.9 0.0 collective-permute-done.4.refs_6_.refs_11_
  26.9 1.0 collective-permute-done.3.refs_5_.refs_10_
  27.9 0.8 collective-permute-done.2.refs_4_.refs_9_
  28.6 0.0 collective-permute-done.1.refs_3_.refs_8_
  28.6 1.5 %collective-permute-done.refs_2_.refs_7_ = f32[64,256]{1,0:T(8,128)S(1)} collective-permute-done((f32[64,256]{1,0:T(8,128)S(1)}, f32[64,256]{1,0:T(8,128)S(1)}, u32[]{:S(2)}, u32[]{:S(2)}) %collective-permute-start) | collective-permute-done | bytes 65568 | tf_op jit(solution)/shard_map/ppermute | solution.py:565
  30.1 3.9 %all-to-all-done.refs_0_ = f32[32,1,4736]{2,1,0:T(1,128)S(1)} async-done(((f32[32,1,4736]{2,1,0:T(1,128)}), f32[32,1,4736]{2,1,0:T(1,128)S(1)}, u32[]{:S(2)}, u32[]{:S(2)}) %all-to-all-start) | async-done | bytes 606240 | tf_op jit(solution)/shard_map/all_to_all | solution.py:569
  34.0 10.9 %forward.1 = (f32[32,128]{1,0:T(8,128)S(1)}, f32[6,24,16,128]{3,2,1,0:T(8,128)S(1)}, f32[24,16,128]{2,1,0:T(8,128)S(1)}, bf16[24,64,2048]{2,1,0:T(8,128)(2,1)S(1)}, s32[27]{0:T(128)S(1)}) custom-call(f32[32,1,4736]{2,1,0:T(1,128)S(1)} %all-to-all-done.refs_0_, f32[64,256]{1,0:T(8,128)S(1)} %maximum_convert_fusion.refs_1_.refs_6_, ...), custom_call_target="tpu_custom_call" | custom-call | flops 12884901888 | bytes 4194304 | tf_op jit(solution)/shard_map/forward/pallas_call | solution.py:349
  44.9 16.1 %all_to_all.43 = f32[32,1,128]{2,1,0:T(1,128)S(1)} all-to-all(f32[32,1,128]{2,1,0:T(1,128)S(1)} %bitcast.25), channel_id=1, replica_groups=mesh['gx'=8,'gy'=4,'gz'=8] {'gx','gy'}, dimensions={0} | all-to-all | bytes 32768 | tf_op jit(solution)/shard_map/all_to_all | solution.py:569
  61.0 0.0 copy-done
  61.0 0.0 copy-done.1
  61.0 0.0 copy-done.2
  61.0 1.9 %rays.1 = (f32[32,128]{1,0:T(8,128)S(1)}, f32[3,48]{1,0:T(4,128)}) custom-call(f32[32,128]{1,0:T(8,128)S(1)} %bitcast.23, f32[384,128]{1,0:T(8,128)S(1)} %copy-done, f32[8,384]{1,0:T(8,128)S(1)} %copy-done.1, f32[3,48]{1,0:T(4,128)S(1)} %copy-done.2), custom_call_target="tpu_custom_call" | custom-call | tf_op jit(solution)/shard_map/rays/pallas_call | solution.py:414
  62.9 11.5 %all_to_all.44 = f32[32,1,128]{2,1,0:T(1,128)S(1)} all-to-all(f32[32,1,128]{2,1,0:T(1,128)S(1)} %bitcast.26), channel_id=1, replica_groups=mesh['gx'=8,'gy'=4,'gz'=8] {'gx','gy'}, dimensions={0} | all-to-all | bytes 32768 | tf_op jit(solution)/shard_map/all_to_all | solution.py:569
  74.4 15.8 %backward.1 = f32[8,64,256]{2,1,0:T(8,128)S(1)} custom-call(s32[1]{0:T(128)} %bitcast.member_ref.refs_0_, f32[32,128]{1,0:T(8,128)S(1)} %bitcast.24, f32[6,24,16,128]{3,2,1,0:T(8,128)S(1)} %get-tuple-element.23.refs_2_, f32[24,16,128]{2,1,0:T(8,128)S(1)} %get-tuple-element.24.refs_3_, bf16[24,64,2048]{2,1,0:T(8,128)(2,1)S(1)} %get-tuple-element.25.refs_4_, ...), custom_call_target="tpu_custom_call" | custom-call | flops 25769803776 | bytes 4194304 | tf_op jit(solution)/shard_map/backward/pallas_call | solution.py:501
  90.3 15.6 %all_to_all.45.refs_0_ = f32[8,64,256]{2,1,0:T(8,128)S(1)} all-to-all(f32[8,64,256]{2,1,0:T(8,128)S(1)} %backward.1), channel_id=1, replica_groups=mesh['gx'=8,'gy'=4,'gz'=8] {'gz'}, dimensions={0} | all-to-all | bytes 1048576 | tf_op jit(solution)/shard_map/all_to_all | solution.py:569
  105.9 0.1 add_up.1
  106.0 22.6 %all_to_all.46 = f32[256,1,128]{2,1,0:T(1,128)S(1)} all-to-all(f32[256,1,128]{2,1,0:T(1,128)S(1)} %bitcast.22), channel_id=1, replica_groups=mesh['gx'=8,'gy'=4,'gz'=8] {'gx','gy','gz'}, dimensions={0} | all-to-all | bytes 262144 | tf_op jit(solution)/shard_map/all_to_all | solution.py:569
  128.7 0.8 normalize.1
  (1 shorter events, 0.0 us)
Async XLA Ops:
  4.3 29.7 %all-to-all-start = ((f32[32,1,4736]{2,1,0:T(1,128)}), f32[32,1,4736]{2,1,0:T(1,128)S(1)}, u32[]{:S(2)}, u32[]{:S(2)}) async-start(f32[32,1,4736]{2,1,0:T(1,128)} %get-tuple-element.17), calls=%async_computation | async-start | bytes 1212416 | tf_op jit(solution)/shard_map/all_to_all | solution.py:569
  17.0 44.0 %copy-start = (f32[384,128]{1,0:T(8,128)S(1)}, f32[384,128]{1,0:T(8,128)}, u32[]{:S(2)}) copy-start(f32[384,128]{1,0:T(8,128)} %get-tuple-element.19.index_ref) | copy-start | bytes 589828
  17.0 44.0 %copy-start.1 = (f32[8,384]{1,0:T(8,128)S(1)}, f32[8,384]{1,0:T(8,128)}, u32[]{:S(2)}) copy-start(f32[8,384]{1,0:T(8,128)} %get-tuple-element.20.dest_ref) | copy-start | bytes 36868
  17.0 44.0 %copy-start.2 = (f32[3,48]{1,0:T(4,128)S(1)}, f32[3,48]{1,0:T(4,128)}, u32[]{:S(2)}) copy-start(f32[3,48]{1,0:T(4,128)} %target_ref.1) | copy-start | bytes 1732
  17.0 7.4 %collective-permute-start.6 = (f32[64,256]{1,0:T(8,128)S(1)}, f32[64,256]{1,0:T(8,128)S(1)}, u32[]{:S(2)}, u32[]{:S(2)}) collective-permute-start(f32[64,256]{1,0:T(8,128)S(1)} %maximum_convert_fusion.refs_1_.refs_6_), channel_id=1, source_target_pairs={{0,1},{1,2},{2,3},{3,4},{4,5},{5,6},{6,7},{7,0},{8,9},{9,10},{10,1... | collective-permute-start | bytes 196616 | tf_op jit(solution)/shard_map/ppermute | solution.py:565
  19.2 6.1 %collective-permute-start.5 = (f32[64,256]{1,0:T(8,128)S(1)}, f32[64,256]{1,0:T(8,128)S(1)}, u32[]{:S(2)}, u32[]{:S(2)}) collective-permute-start(f32[64,256]{1,0:T(8,128)S(1)} %maximum_convert_fusion.refs_1_.refs_6_), channel_id=1, source_target_pairs={{0,2},{1,3},{2,4},{3,5},{4,6},{5,7},{6,0},{7,1},{8,10},{9,11},{10,... | collective-permute-start | bytes 196616 | tf_op jit(solution)/shard_map/ppermute | solution.py:565
  20.4 6.4 %collective-permute-start.4 = (f32[64,256]{1,0:T(8,128)S(1)}, f32[64,256]{1,0:T(8,128)S(1)}, u32[]{:S(2)}, u32[]{:S(2)}) collective-permute-start(f32[64,256]{1,0:T(8,128)S(1)} %maximum_convert_fusion.refs_1_.refs_6_), channel_id=1, source_target_pairs={{0,3},{1,4},{2,5},{3,6},{4,7},{5,0},{6,1},{7,2},{8,11},{9,12},{10,... | collective-permute-start | bytes 196616 | tf_op jit(solution)/shard_map/ppermute | solution.py:565
  22.1 5.7 %collective-permute-start.3 = (f32[64,256]{1,0:T(8,128)S(1)}, f32[64,256]{1,0:T(8,128)S(1)}, u32[]{:S(2)}, u32[]{:S(2)}) collective-permute-start(f32[64,256]{1,0:T(8,128)S(1)} %maximum_convert_fusion.refs_1_.refs_6_), channel_id=1, source_target_pairs={{0,4},{1,5},{2,6},{3,7},{4,0},{5,1},{6,2},{7,3},{8,12},{9,13},{10,... | collective-permute-start | bytes 196616 | tf_op jit(solution)/shard_map/ppermute | solution.py:565
  22.5 6.1 %collective-permute-start.2 = (f32[64,256]{1,0:T(8,128)S(1)}, f32[64,256]{1,0:T(8,128)S(1)}, u32[]{:S(2)}, u32[]{:S(2)}) collective-permute-start(f32[64,256]{1,0:T(8,128)S(1)} %maximum_convert_fusion.refs_1_.refs_6_), channel_id=1, source_target_pairs={{0,5},{1,6},{2,7},{3,0},{4,1},{5,2},{6,3},{7,4},{8,13},{9,14},{10,... | collective-permute-start | bytes 196616 | tf_op jit(solution)/shard_map/ppermute | solution.py:565
  24.4 4.2 %collective-permute-start.1 = (f32[64,256]{1,0:T(8,128)S(1)}, f32[64,256]{1,0:T(8,128)S(1)}, u32[]{:S(2)}, u32[]{:S(2)}) collective-permute-start(f32[64,256]{1,0:T(8,128)S(1)} %maximum_convert_fusion.refs_1_.refs_6_), channel_id=1, source_target_pairs={{0,6},{1,7},{2,0},{3,1},{4,2},{5,3},{6,4},{7,5},{8,14},{9,15},{10,... | collective-permute-start | bytes 196616 | tf_op jit(solution)/shard_map/ppermute | solution.py:565
  25.3 4.8 %collective-permute-start = (f32[64,256]{1,0:T(8,128)S(1)}, f32[64,256]{1,0:T(8,128)S(1)}, u32[]{:S(2)}, u32[]{:S(2)}) collective-permute-start(f32[64,256]{1,0:T(8,128)S(1)} %maximum_convert_fusion.refs_1_.refs_6_), channel_id=1, source_target_pairs={{0,7},{1,0},{2,1},{3,2},{4,3},{5,4},{6,5},{7,6},{8,15},{9,8},{10,9... | collective-permute-start | bytes 196616 | tf_op jit(solution)/shard_map/ppermute | solution.py:565

commit v4 on v3

--- a/solution.py
+++ b/solution.py
@@ -224,19 +224,24 @@
         kept_ref[slot, :, lanes] = waves
 
 
-def in_turns(used_ref, count, prepare, work, buffers):
+def in_turns(used_ref, count, prepare, work, buffers, work_first=False):
     here, other = buffers
     prepare(here, used_ref[0])
 
+    def both(empty, later, full, now):
+        if work_first:
+            work(full, now)
+        prepare(empty, later)
+        if not work_first:
+            work(full, now)
+
     def turn(number, carry):
         place = 2 * number
-        prepare(other, used_ref[place + 1])
-        work(here, used_ref[place])
+        both(other, used_ref[place + 1], here, used_ref[place])
 
         @pl.when(place + 1 < count)
         def _():
-            prepare(here, used_ref[place + 2])
-            work(other, used_ref[place + 1])
+            both(here, used_ref[place + 2], other, used_ref[place + 1])
 
         return carry
 
@@ -312,7 +317,7 @@
     def prepare(ref, slot):
         encode_into(ref, kept_ref, wave_ref, recv_ref, slot)
 
-    in_turns(used_ref, count, prepare, network, (enc_ref, next_ref))
+    in_turns(used_ref, count, prepare, network, (enc_ref, next_ref), work_first=True)
 
     rows = SLOTS * ROWS
     outputs = [out_ref[v].reshape(rows, 128) for v in range(4)]

time: 130 us -> 130 us (level)
  Pallas kernels: 33.2 us -> 31.2 us
  blocking collectives: 65.9 us -> 67.9 us
    all_to_all x4, blocking collectives: 65.9 us -> 67.9 us  [exchange(): return lax.all_to_all(x, axes, split_axis=0, concat_axis=0, tiled=True)]
where the time goes in v4:
time: 130 us; the launch traced here: 129 us
  blocking collectives  67.9 us (52%)
  Pallas kernels  31.2 us (24%)
  starting transfers between devices  21.7 us (17%)
  waiting for transfers between devices  7.14 us (5%)
    all_to_all x4, blocking collectives, exchange(): return lax.all_to_all(x, axes, split_axis=0, concat_axis=0, tiled=True)  67.9 us
    pallas_call x1, Pallas kernels, backward(): pl.pallas_call(backward_kernel, out_shape=jax.ShapeDtypeStruct((GROUP, 64...  14.8 us
    all_to_all x1, starting transfers between devices, exchange(): return lax.all_to_all(x, axes, split_axis=0, concat_axis=0, tiled=True)  11.9 us
    pallas_call x1, Pallas kernels, forward(): pl.pallas_call(forward_kernel, out_shape=(jax.ShapeDtypeStruct((PEERS, 12...  10.1 us
    ppermute x7, starting transfers between devices, from_ahead(): lax.ppermute(x, GROUP_AXIS, [(i, (i - distance) % GROUP) for i in range(G...  9.85 us
    all_to_all x1, waiting for transfers between devices, exchange(): return lax.all_to_all(x, axes, split_axis=0, concat_axis=0, tiled=True)  3.92 us
    pallas_call x1, Pallas kernels, pack(): pl.pallas_call(pack_kernel, out_shape=(jax.ShapeDtypeStruct((PEERS, 1, 12...  3.68 us
    ppermute x7, waiting for transfers between devices, from_ahead(): lax.ppermute(x, GROUP_AXIS, [(i, (i - distance) % GROUP) for i in range(G...  3.22 us
  transfers between devices with their start and end apart: 8, of which 4 were waited for; matrix products, arithmetic and copies ran while one was open for 1% of the time, Pallas kernels for 0%

profile of v4, /device:TPU:1, one launch (start us, length us, event | category | flops | bytes accessed | tf_op | source)
XLA Modules:
  0.0 129.5 jit_solution(12083407989910109556)
XLA Ops:
  0.6 3.7 %pack.1 = (f32[32,1,4736]{2,1,0:T(1,128)}, f32[384,128]{1,0:T(8,128)}, f32[8,384]{1,0:T(8,128)}) custom-call(s32[1]{0:T(128)} %bitcast.member_ref.refs_0_, s32[1]{0:T(128)} %bitcast.1.peer_ref, f32[3,48,512]{2,1,0:T(8,128)} %pos_ref.1, f32[8,48]{1,0:T(8,128)} %bitcast.28, s32[8,48]{1,0:T(8,128)} %bitcast.29), custom_call_target="tpu_custom_call" | custom-call | tf_op jit(solution)/shard_map/pack/pallas_call | solution.py:163
  4.3 11.9 %all-to-all-start = ((f32[32,1,4736]{2,1,0:T(1,128)}), f32[32,1,4736]{2,1,0:T(1,128)S(1)}, u32[]{:S(2)}, u32[]{:S(2)}) async-start(f32[32,1,4736]{2,1,0:T(1,128)} %get-tuple-element.17), calls=%async_computation | async-start | bytes 1212416 | tf_op jit(solution)/shard_map/all_to_all | solution.py:574
  16.2 0.8 maximum_convert_fusion.refs_1_.refs_6_
  17.0 0.0 copy-start.1
  17.0 0.0 copy-start.2
  17.0 2.1 %collective-permute-start.6 = (f32[64,256]{1,0:T(8,128)S(1)}, f32[64,256]{1,0:T(8,128)S(1)}, u32[]{:S(2)}, u32[]{:S(2)}) collective-permute-start(f32[64,256]{1,0:T(8,128)S(1)} %maximum_convert_fusion.refs_1_.refs_6_), channel_id=1, source_target_pairs={{0,1},{1,2},{2,3},{3,4},{4,5},{5,6},{6,7},{7,0},{8,9},{9,10},{10,1... | collective-permute-start | bytes 196616 | tf_op jit(solution)/shard_map/ppermute | solution.py:570
  19.2 1.3 %collective-permute-start.5 = (f32[64,256]{1,0:T(8,128)S(1)}, f32[64,256]{1,0:T(8,128)S(1)}, u32[]{:S(2)}, u32[]{:S(2)}) collective-permute-start(f32[64,256]{1,0:T(8,128)S(1)} %maximum_convert_fusion.refs_1_.refs_6_), channel_id=1, source_target_pairs={{0,2},{1,3},{2,4},{3,5},{4,6},{5,7},{6,0},{7,1},{8,10},{9,11},{10,... | collective-permute-start | bytes 196616 | tf_op jit(solution)/shard_map/ppermute | solution.py:570
  20.4 1.7 %collective-permute-start.4 = (f32[64,256]{1,0:T(8,128)S(1)}, f32[64,256]{1,0:T(8,128)S(1)}, u32[]{:S(2)}, u32[]{:S(2)}) collective-permute-start(f32[64,256]{1,0:T(8,128)S(1)} %maximum_convert_fusion.refs_1_.refs_6_), channel_id=1, source_target_pairs={{0,3},{1,4},{2,5},{3,6},{4,7},{5,0},{6,1},{7,2},{8,11},{9,12},{10,... | collective-permute-start | bytes 196616 | tf_op jit(solution)/shard_map/ppermute | solution.py:570
  22.1 0.3 collective-permute-start.3
  22.5 1.9 %collective-permute-start.2 = (f32[64,256]{1,0:T(8,128)S(1)}, f32[64,256]{1,0:T(8,128)S(1)}, u32[]{:S(2)}, u32[]{:S(2)}) collective-permute-start(f32[64,256]{1,0:T(8,128)S(1)} %maximum_convert_fusion.refs_1_.refs_6_), channel_id=1, source_target_pairs={{0,5},{1,6},{2,7},{3,0},{4,1},{5,2},{6,3},{7,4},{8,13},{9,14},{10,... | collective-permute-start | bytes 196616 | tf_op jit(solution)/shard_map/ppermute | solution.py:570
  24.4 0.0 collective-permute-done.6.refs_8_.refs_13_
  24.4 0.8 collective-permute-start.1
  25.3 0.0 collective-permute-done.5.refs_7_.refs_12_
  25.3 1.6 %collective-permute-start = (f32[64,256]{1,0:T(8,128)S(1)}, f32[64,256]{1,0:T(8,128)S(1)}, u32[]{:S(2)}, u32[]{:S(2)}) collective-permute-start(f32[64,256]{1,0:T(8,128)S(1)} %maximum_convert_fusion.refs_1_.refs_6_), channel_id=1, source_target_pairs={{0,7},{1,0},{2,1},{3,2},{4,3},{5,4},{6,5},{7,6},{8,15},{9,8},{10,9... | collective-permute-start | bytes 196616 | tf_op jit(solution)/shard_map/ppermute | solution.py:570
  26.9 0.0 collective-permute-done.4.refs_6_.refs_11_
  26.9 1.0 collective-permute-done.3.refs_5_.refs_10_
  27.9 0.8 collective-permute-done.2.refs_4_.refs_9_
  28.6 0.0 collective-permute-done.1.refs_3_.refs_8_
  28.6 1.5 %collective-permute-done.refs_2_.refs_7_ = f32[64,256]{1,0:T(8,128)S(1)} collective-permute-done((f32[64,256]{1,0:T(8,128)S(1)}, f32[64,256]{1,0:T(8,128)S(1)}, u32[]{:S(2)}, u32[]{:S(2)}) %collective-permute-start) | collective-permute-done | bytes 65568 | tf_op jit(solution)/shard_map/ppermute | solution.py:570
  30.1 3.9 %all-to-all-done.refs_0_ = f32[32,1,4736]{2,1,0:T(1,128)S(1)} async-done(((f32[32,1,4736]{2,1,0:T(1,128)}), f32[32,1,4736]{2,1,0:T(1,128)S(1)}, u32[]{:S(2)}, u32[]{:S(2)}) %all-to-all-start) | async-done | bytes 606240 | tf_op jit(solution)/shard_map/all_to_all | solution.py:574
  34.0 10.1 %forward.1 = (f32[32,128]{1,0:T(8,128)S(1)}, f32[6,24,16,128]{3,2,1,0:T(8,128)S(1)}, f32[24,16,128]{2,1,0:T(8,128)S(1)}, bf16[24,64,2048]{2,1,0:T(8,128)(2,1)S(1)}, s32[27]{0:T(128)S(1)}) custom-call(f32[32,1,4736]{2,1,0:T(1,128)S(1)} %all-to-all-done.refs_0_, f32[64,256]{1,0:T(8,128)S(1)} %maximum_convert_fusion.refs_1_.refs_6_, ...), custom_call_target="tpu_custom_call" | custom-call | flops 12884901888 | bytes 4194304 | tf_op jit(solution)/shard_map/forward/pallas_call | solution.py:354
  44.1 16.1 %all_to_all.43 = f32[32,1,128]{2,1,0:T(1,128)S(1)} all-to-all(f32[32,1,128]{2,1,0:T(1,128)S(1)} %bitcast.25), channel_id=1, replica_groups=mesh['gx'=8,'gy'=4,'gz'=8] {'gx','gy'}, dimensions={0} | all-to-all | bytes 32768 | tf_op jit(solution)/shard_map/all_to_all | solution.py:574
  60.1 0.0 copy-done
  60.1 0.0 copy-done.1
  60.1 0.0 copy-done.2
  60.1 1.9 %rays.1 = (f32[32,128]{1,0:T(8,128)S(1)}, f32[3,48]{1,0:T(4,128)}) custom-call(f32[32,128]{1,0:T(8,128)S(1)} %bitcast.23, f32[384,128]{1,0:T(8,128)S(1)} %copy-done, f32[8,384]{1,0:T(8,128)S(1)} %copy-done.1, f32[3,48]{1,0:T(4,128)S(1)} %copy-done.2), custom_call_target="tpu_custom_call" | custom-call | tf_op jit(solution)/shard_map/rays/pallas_call | solution.py:419
  62.0 11.5 %all_to_all.44 = f32[32,1,128]{2,1,0:T(1,128)S(1)} all-to-all(f32[32,1,128]{2,1,0:T(1,128)S(1)} %bitcast.26), channel_id=1, replica_groups=mesh['gx'=8,'gy'=4,'gz'=8] {'gx','gy'}, dimensions={0} | all-to-all | bytes 32768 | tf_op jit(solution)/shard_map/all_to_all | solution.py:574
  73.6 14.8 %backward.1 = f32[8,64,256]{2,1,0:T(8,128)S(1)} custom-call(s32[1]{0:T(128)} %bitcast.member_ref.refs_0_, f32[32,128]{1,0:T(8,128)S(1)} %bitcast.24, f32[6,24,16,128]{3,2,1,0:T(8,128)S(1)} %get-tuple-element.23.refs_2_, f32[24,16,128]{2,1,0:T(8,128)S(1)} %get-tuple-element.24.refs_3_, bf16[24,64,2048]{2,1,0:T(8,128)(2,1)S(1)} %get-tuple-element.25.refs_4_, ...), custom_call_target="tpu_custom_call" | custom-call | flops 25769803776 | bytes 4194304 | tf_op jit(solution)/shard_map/backward/pallas_call | solution.py:506
  88.3 18.1 %all_to_all.45.refs_0_ = f32[8,64,256]{2,1,0:T(8,128)S(1)} all-to-all(f32[8,64,256]{2,1,0:T(8,128)S(1)} %backward.1), channel_id=1, replica_groups=mesh['gx'=8,'gy'=4,'gz'=8] {'gz'}, dimensions={0} | all-to-all | bytes 1048576 | tf_op jit(solution)/shard_map/all_to_all | solution.py:574
  106.4 0.1 add_up.1
  106.6 22.2 %all_to_all.46 = f32[256,1,128]{2,1,0:T(1,128)S(1)} all-to-all(f32[256,1,128]{2,1,0:T(1,128)S(1)} %bitcast.22), channel_id=1, replica_groups=mesh['gx'=8,'gy'=4,'gz'=8] {'gx','gy','gz'}, dimensions={0} | all-to-all | bytes 262144 | tf_op jit(solution)/shard_map/all_to_all | solution.py:574
  128.7 0.8 normalize.1
  (1 shorter events, 0.0 us)
Async XLA Ops:
  4.3 29.7 %all-to-all-start = ((f32[32,1,4736]{2,1,0:T(1,128)}), f32[32,1,4736]{2,1,0:T(1,128)S(1)}, u32[]{:S(2)}, u32[]{:S(2)}) async-start(f32[32,1,4736]{2,1,0:T(1,128)} %get-tuple-element.17), calls=%async_computation | async-start | bytes 1212416 | tf_op jit(solution)/shard_map/all_to_all | solution.py:574
  17.0 43.2 %copy-start = (f32[384,128]{1,0:T(8,128)S(1)}, f32[384,128]{1,0:T(8,128)}, u32[]{:S(2)}) copy-start(f32[384,128]{1,0:T(8,128)} %get-tuple-element.19.index_ref) | copy-start | bytes 589828
  17.0 43.2 %copy-start.1 = (f32[8,384]{1,0:T(8,128)S(1)}, f32[8,384]{1,0:T(8,128)}, u32[]{:S(2)}) copy-start(f32[8,384]{1,0:T(8,128)} %get-tuple-element.20.dest_ref) | copy-start | bytes 36868
  17.0 43.2 %copy-start.2 = (f32[3,48]{1,0:T(4,128)S(1)}, f32[3,48]{1,0:T(4,128)}, u32[]{:S(2)}) copy-start(f32[3,48]{1,0:T(4,128)} %target_ref.1) | copy-start | bytes 1732
  17.0 7.4 %collective-permute-start.6 = (f32[64,256]{1,0:T(8,128)S(1)}, f32[64,256]{1,0:T(8,128)S(1)}, u32[]{:S(2)}, u32[]{:S(2)}) collective-permute-start(f32[64,256]{1,0:T(8,128)S(1)} %maximum_convert_fusion.refs_1_.refs_6_), channel_id=1, source_target_pairs={{0,1},{1,2},{2,3},{3,4},{4,5},{5,6},{6,7},{7,0},{8,9},{9,10},{10,1... | collective-permute-start | bytes 196616 | tf_op jit(solution)/shard_map/ppermute | solution.py:570
  19.2 6.1 %collective-permute-start.5 = (f32[64,256]{1,0:T(8,128)S(1)}, f32[64,256]{1,0:T(8,128)S(1)}, u32[]{:S(2)}, u32[]{:S(2)}) collective-permute-start(f32[64,256]{1,0:T(8,128)S(1)} %maximum_convert_fusion.refs_1_.refs_6_), channel_id=1, source_target_pairs={{0,2},{1,3},{2,4},{3,5},{4,6},{5,7},{6,0},{7,1},{8,10},{9,11},{10,... | collective-permute-start | bytes 196616 | tf_op jit(solution)/shard_map/ppermute | solution.py:570
  20.4 6.4 %collective-permute-start.4 = (f32[64,256]{1,0:T(8,128)S(1)}, f32[64,256]{1,0:T(8,128)S(1)}, u32[]{:S(2)}, u32[]{:S(2)}) collective-permute-start(f32[64,256]{1,0:T(8,128)S(1)} %maximum_convert_fusion.refs_1_.refs_6_), channel_id=1, source_target_pairs={{0,3},{1,4},{2,5},{3,6},{4,7},{5,0},{6,1},{7,2},{8,11},{9,12},{10,... | collective-permute-start | bytes 196616 | tf_op jit(solution)/shard_map/ppermute | solution.py:570
  22.1 5.7 %collective-permute-start.3 = (f32[64,256]{1,0:T(8,128)S(1)}, f32[64,256]{1,0:T(8,128)S(1)}, u32[]{:S(2)}, u32[]{:S(2)}) collective-permute-start(f32[64,256]{1,0:T(8,128)S(1)} %maximum_convert_fusion.refs_1_.refs_6_), channel_id=1, source_target_pairs={{0,4},{1,5},{2,6},{3,7},{4,0},{5,1},{6,2},{7,3},{8,12},{9,13},{10,... | collective-permute-start | bytes 196616 | tf_op jit(solution)/shard_map/ppermute | solution.py:570
  22.5 6.1 %collective-permute-start.2 = (f32[64,256]{1,0:T(8,128)S(1)}, f32[64,256]{1,0:T(8,128)S(1)}, u32[]{:S(2)}, u32[]{:S(2)}) collective-permute-start(f32[64,256]{1,0:T(8,128)S(1)} %maximum_convert_fusion.refs_1_.refs_6_), channel_id=1, source_target_pairs={{0,5},{1,6},{2,7},{3,0},{4,1},{5,2},{6,3},{7,4},{8,13},{9,14},{10,... | collective-permute-start | bytes 196616 | tf_op jit(solution)/shard_map/ppermute | solution.py:570
  24.4 4.2 %collective-permute-start.1 = (f32[64,256]{1,0:T(8,128)S(1)}, f32[64,256]{1,0:T(8,128)S(1)}, u32[]{:S(2)}, u32[]{:S(2)}) collective-permute-start(f32[64,256]{1,0:T(8,128)S(1)} %maximum_convert_fusion.refs_1_.refs_6_), channel_id=1, source_target_pairs={{0,6},{1,7},{2,0},{3,1},{4,2},{5,3},{6,4},{7,5},{8,14},{9,15},{10,... | collective-permute-start | bytes 196616 | tf_op jit(solution)/shard_map/ppermute | solution.py:570
  25.3 4.8 %collective-permute-start = (f32[64,256]{1,0:T(8,128)S(1)}, f32[64,256]{1,0:T(8,128)S(1)}, u32[]{:S(2)}, u32[]{:S(2)}) collective-permute-start(f32[64,256]{1,0:T(8,128)S(1)} %maximum_convert_fusion.refs_1_.refs_6_), channel_id=1, source_target_pairs={{0,7},{1,0},{2,1},{3,2},{4,3},{5,4},{6,5},{7,6},{8,15},{9,8},{10,9... | collective-permute-start | bytes 196616 | tf_op jit(solution)/shard_map/ppermute | solution.py:570
